TPU v7x, 32 devices: a whole 2x2x4 slice. The times are simulated.
32 devices in a mesh: hst: 4 (over z), dev: 8 (over y, x, core).
Axes of the slice: x: 2, y: 2, z: 4, core: 2. Of those that a mesh axis runs over, the one named last changes fastest.
Arguments:
- features: bfloat16 [65536, 768], P(('hst', 'dev')), may hold values from -6 to 6
- cache_blocks: bfloat16 [4, 2048, 768], P('hst', 'dev'), may hold values from -6 to 6
- plan: int32 [4, 16], P('hst', 'dev'), may hold values from 0 to 15, as said below
- miss_ids: int32 [32, 4, 8, 64], P(('hst', 'dev')), may hold values from 0 to 2303, as said below
- miss_counts: int32 [32, 4, 8], P(('hst', 'dev')), may hold values from 16 to 64, as said below
- self_ids: int32 [26624], P(('hst', 'dev')), may hold values from 0 to 2047, as said below
- nbr_ids: int32 [26624, 15], P(('hst', 'dev')), may hold values from 0 to 2047, as said below
- hop_counts: int32 [26624], P(('hst', 'dev')), may hold values from 1 to 15, as said below
- seed_counts: int32 [1024], P(('hst', 'dev')), may hold values from 1 to 25, as said below
- w_self1: bfloat16 [768, 1024], replicated, may hold values from -0.21875 to 0.21875
- w_nbr1: bfloat16 [768, 1024], replicated, may hold values from -0.21875 to 0.21875
- w_self2: bfloat16 [1024, 1024], replicated, may hold values from -0.1875 to 0.1875
- w_nbr2: bfloat16 [1024, 1024], replicated, may hold values from -0.1875 to 0.1875
- cotangent: bfloat16 [1024, 1024], P(('hst', 'dev')), may hold values from -0.29882812 to 0.29882812
Outputs:
- embedding: bfloat16 [1024, 1024], P(('hst', 'dev'))
- new_cache: bfloat16 [4, 2048, 768], P('hst', 'dev')
- grad_self1: float32 [768, 1024], P(None, ('hst', 'dev'))
- grad_nbr1: float32 [768, 1024], P(None, ('hst', 'dev'))
- grad_self2: float32 [1024, 1024], P(None, ('hst', 'dev'))
- grad_nbr2: float32 [1024, 1024], P(None, ('hst', 'dev'))
Inputs may be any that keep to these rules, and one draw needn't show every extreme that they name: Within each cache domain h, plan[h] is a permutation of the 16 block numbers. `miss_ids`: row numbers into the peer's served table; slots at or past the count are unused. `miss_counts`: in every draw some peer is asked for 64 rows by every device. `self_ids`: each names a used fetched slot p * 64 + c of the same device, c below that device's count for peer p. `nbr_ids`: each names a used fetched slot p * 64 + c of the same device, c below that device's count for peer p. `hop_counts`: the first node of every device has 15. `seed_counts`: the first seed of every device has 25.
All inputs are finite; a program needn't handle non-finite values.
Results may differ from a plain program's by a relative error of at most 0.0052.
Values may be sent and summed in bfloat16 or wider, within the bound.
A program may use at most 128 MiB of HBM per device.

v0:
```python
import jax
import jax.numpy as jnp
from jax import lax
from jax.sharding import PartitionSpec as P

FAN1 = 25
FAN2 = 15
CSLOT = 2
BLOCK = 128


def local_step(
    frontier, self_rows, nbr_rows, count_one, count_two, w_self1, w_nbr1, w_self2, w_nbr2, cot_rows
):
    seed_count = count_two.shape[0]
    width = w_self2.shape[0]
    width_in = frontier.shape[1]
    own_rows = frontier[self_rows]
    mask_one = jnp.arange(FAN2, dtype=jnp.int32)[None, :] < count_one[:, None]
    summed_one = jnp.zeros((own_rows.shape[0], width_in), jnp.float32)
    for k in range(FAN2):
        picked = frontier[nbr_rows[:, k]].astype(jnp.float32)
        summed_one = summed_one + jnp.where(mask_one[:, k][:, None], picked, jnp.zeros_like(picked))
    mean_one = (summed_one / count_one[:, None].astype(jnp.float32)).astype(jnp.bfloat16)
    hidden_pre = jnp.dot(own_rows, w_self1, preferred_element_type=jnp.float32) + jnp.dot(
        mean_one, w_nbr1, preferred_element_type=jnp.float32
    )
    hidden_one = jax.nn.silu(hidden_pre).astype(jnp.bfloat16)
    seed_rows = hidden_one[:seed_count]
    hop_rows = hidden_one[seed_count:].reshape(seed_count, FAN1, width)
    mask_two = jnp.arange(FAN1, dtype=jnp.int32)[None, :] < count_two[:, None]
    summed_two = jnp.einsum(
        "skh,sk->sh", hop_rows, mask_two.astype(jnp.bfloat16), preferred_element_type=jnp.float32
    )
    mean_two = (summed_two / count_two[:, None].astype(jnp.float32)).astype(jnp.bfloat16)
    embedding = (
        jnp.dot(seed_rows, w_self2, preferred_element_type=jnp.float32)
        + jnp.dot(mean_two, w_nbr2, preferred_element_type=jnp.float32)
    ).astype(jnp.bfloat16)
    grad_self2 = jnp.dot(cot_rows.T, seed_rows, preferred_element_type=jnp.float32)
    grad_nbr2 = jnp.dot(cot_rows.T, mean_two, preferred_element_type=jnp.float32)
    back_self = jnp.dot(cot_rows, w_self2.T, preferred_element_type=jnp.float32)
    back_mean = jnp.dot(cot_rows, w_nbr2.T, preferred_element_type=jnp.float32) / count_two[
        :, None
    ].astype(jnp.float32)
    back_hop = back_mean[:, None, :] * mask_two.astype(jnp.float32)[:, :, None]
    back_hidden = jnp.concatenate([back_self, back_hop.reshape(seed_count * FAN1, width)], 0)
    gate_value = jax.nn.sigmoid(hidden_pre)
    back_pre = (back_hidden * gate_value * (1.0 + hidden_pre * (1.0 - gate_value))).astype(
        jnp.bfloat16
    )
    grad_self1 = jnp.dot(back_pre.T, own_rows, preferred_element_type=jnp.float32)
    grad_nbr1 = jnp.dot(back_pre.T, mean_one, preferred_element_type=jnp.float32)
    return (embedding, (grad_self1, grad_nbr1, grad_self2, grad_nbr2))


def local(
    features,
    cache_blocks,
    plan,
    miss_ids,
    miss_counts,
    self_ids,
    nbr_ids,
    hop_counts,
    seed_counts,
    w_self1,
    w_nbr1,
    w_self2,
    w_nbr2,
    cotangent,
):
    width_in = features.shape[1]
    slot_count = miss_ids.shape[3]
    device_count = lax.axis_size(("hst", "dev"))
    start_cache = jnp.zeros((CSLOT, BLOCK, width_in), jnp.bfloat16)
    current = start_cache
    shard_rows = lax.all_gather(cache_blocks, "dev", axis=1, tiled=True)
    block_count = shard_rows.shape[1] // BLOCK
    arrived = shard_rows[0].reshape(block_count, BLOCK, width_in)
    for target in range(CSLOT):
        offset = plan[0, target]
        inside = (offset >= 0) & (offset < block_count)
        chosen = lax.dynamic_index_in_dim(
            arrived, jnp.clip(offset, 0, block_count - 1), 0, keepdims=False
        )
        current = current.at[target].set(jnp.where(inside, chosen, current[target]))
    new_cache = current.reshape(1, CSLOT * BLOCK, width_in)
    lookup_table = jnp.concatenate([features, new_cache[0]], 0)
    requests = miss_ids.reshape(device_count, slot_count)
    row_data = lookup_table[
        lax.all_to_all(requests, ("hst", "dev"), split_axis=0, concat_axis=0, tiled=True)
    ]
    fetched = lax.all_to_all(row_data, ("hst", "dev"), split_axis=0, concat_axis=0, tiled=True)
    counted = miss_counts.reshape(device_count)
    is_valid = jnp.arange(slot_count, dtype=jnp.int32)[None, :] < counted[:, None]
    fetched = jnp.where(is_valid[:, :, None], fetched, jnp.zeros_like(fetched))
    frontier = fetched.reshape(device_count * slot_count, width_in)
    embedding, grads = local_step(
        frontier,
        self_ids,
        nbr_ids,
        hop_counts,
        seed_counts,
        w_self1,
        w_nbr1,
        w_self2,
        w_nbr2,
        cotangent,
    )
    share_self1, share_nbr1, share_self2, share_nbr2 = (
        lax.psum_scatter(grads[0], ("hst", "dev"), scatter_dimension=0, tiled=True),
        lax.psum_scatter(grads[1], ("hst", "dev"), scatter_dimension=0, tiled=True),
        lax.psum_scatter(grads[2], ("hst", "dev"), scatter_dimension=0, tiled=True),
        lax.psum_scatter(grads[3], ("hst", "dev"), scatter_dimension=0, tiled=True),
    )
    return (embedding, new_cache, share_self1.T, share_nbr1.T, share_self2.T, share_nbr2.T)


def solution(mesh):
    return jax.shard_map(
        local,
        mesh=mesh,
        in_specs=(
            P(("hst", "dev"), None),
            P("hst", "dev", None),
            P("hst", "dev"),
            P(("hst", "dev"), None, None, None),
            P(("hst", "dev"), None, None),
            P(("hst", "dev")),
            P(("hst", "dev"), None),
            P(("hst", "dev")),
            P(("hst", "dev")),
            P(),
            P(),
            P(),
            P(),
            P(("hst", "dev"), None),
        ),
        out_specs=(
            P(("hst", "dev"), None),
            P("hst", "dev", None),
            P(None, ("hst", "dev")),
            P(None, ("hst", "dev")),
            P(None, ("hst", "dev")),
            P(None, ("hst", "dev")),
        ),
        check_vma=False,
    )
```

profile of v0, /device:TPU:0, one launch (start us, length us, event | category | flops | bytes accessed | tf_op | source)
XLA Modules:
  0.0 775.0 jit_solution(14992107212309009381)
XLA Ops:
  7.9 7.3 all-to-all-start
  22.4 22.6 %all-gather.2.cloned.1.call-done = bf16[1,2048,768]{2,1,0:T(8,128)(2,1)} async-done(((bf16[1,256,768]{2,1,0:T(8,128)(2,1)}), bf16[1,2048,768]{2,1,0:T(8,128)(2,1)}) %all-gather.2.cloned.1.call-update) | async-done | bytes 3145744 | tf_op jit(solution)/shard_map/all_gather | solution.py:78
  46.8 3.9 pad_maximum_fusion
  50.7 12.6 %gather_fusion = bf16[2048,768]{1,0:T(8,128)(2,1)} fusion(bf16[2304,768]{1,0:T(8,128)(2,1)} %pad_maximum_fusion, s32[2048]{0:T(1024)S(1)} %broadcast_clamp_fusion), kind=kCustom, calls=%fused_computation | custom fusion | bytes 6299648 | tf_op jit(solution)/shard_map/gather | solution.py:91
  63.2 4.7 all-to-all-start.1
  79.6 3.9 broadcast_multiply_fusion
  83.5 55.9 %all-to-all-done.1 = bf16[32,64,768]{2,1,0:T(8,128)(2,1)} async-done(((bf16[32,64,768]{2,1,0:T(8,128)(2,1)}), bf16[32,64,768]{2,1,0:T(8,128)(2,1)}, u32[]{:S(2)}, u32[]{:S(2)}) %all-to-all-start.1) | async-done | bytes 3145760 | tf_op jit(solution)/shard_map/all_to_all | solution.py:94
  142.7 6.7 gather_fusion.10
  149.4 7.1 gather_fusion.11
  156.5 7.1 gather_fusion.12
  163.6 7.1 gather_fusion.13
  170.7 7.1 gather_fusion.14
  177.7 7.1 gather_fusion.15
  184.8 7.1 gather_fusion.16
  191.9 7.3 gather_fusion.3
  199.2 7.1 gather_fusion.4
  206.2 7.1 gather_fusion.5
  213.3 7.1 gather_fusion.6
  220.4 7.1 gather_fusion.7
  227.5 7.1 gather_fusion.8
  234.5 7.1 gather_fusion.9
  241.6 7.1 gather_fusion.2
  248.7 7.3 gather_fusion.1
  260.5 8.8 %divide_convert_fusion = bf16[832,768]{1,0:T(8,128)(2,1)S(1)} fusion(bf16[832,768]{1,0:T(8,128)(2,1)S(1)} %copy-done.7, bf16[832,768]{1,0:T(8,128)(2,1)S(1)} %copy-done.6, bf16[832,768]{1,0:T(8,128)(2,1)S(1)} %copy-done.5, bf16[832,768]{1,0:T(8,128)(2,1)S(1)} %copy-done.4, bf16[832,768]{1,0:T(8,128)(2,1)S(1)} %copy-done.3, ...), kind=kLoop, calls=%fused_computation.24 | loop fusion | flops 29392896 | bytes 20463040 | tf_op jit(solution)/shard_map/convert_element_type | solution.py:24
  269.3 3.9 fusion.1
  279.2 5.1 fusion.31
  294.7 5.4 copy.30
  303.8 5.4 copy.28
  312.0 67.0 %reduce-scatter.11.cloned.1.call-done = f32[32,768]{1,0:T(8,128)} async-done(((f32[1024,768]{1,0:T(8,128)}), f32[32,768]{1,0:T(8,128)}) %reduce-scatter.11.cloned.1.call-update) | async-done | bytes 98320 | tf_op jit(solution)/shard_map/reduce_scatter | solution.py:113
  379.0 106.5 %reduce-scatter.9.cloned.1.call-done = f32[32,768]{1,0:T(8,128)} async-done(((f32[1024,768]{1,0:T(8,128)}), f32[32,768]{1,0:T(8,128)}) %reduce-scatter.9.cloned.1.call-update) | async-done | bytes 98320 | tf_op jit(solution)/shard_map/reduce_scatter | solution.py:112
  485.5 143.0 %reduce-scatter.15.cloned.1.call-done = f32[32,1024]{1,0:T(8,128)} async-done(((f32[1024,1024]{1,0:T(8,128)}), f32[32,1024]{1,0:T(8,128)}) %reduce-scatter.15.cloned.1.call-update) | async-done | bytes 131088
  628.6 139.5 %reduce-scatter.13.cloned.1.call-done = f32[32,1024]{1,0:T(8,128)} async-done(((f32[1024,1024]{1,0:T(8,128)}), f32[32,1024]{1,0:T(8,128)}) %reduce-scatter.13.cloned.1.call-update) | async-done | bytes 131088
  (104 shorter events, 47.7 us)
Async XLA Ops:
  7.2 71.0 %copy-start = (bf16[1024,1024]{1,0:T(8,128)(2,1)S(1)}, bf16[1024,1024]{1,0:T(8,128)(2,1)}, u32[]{:S(2)}) copy-start(bf16[1024,1024]{1,0:T(8,128)(2,1)} %param.29) | copy-start | bytes 6291460
  7.2 37.8 %all-gather.2.cloned.1.call-start = ((), (), s32[]{:S(2)}) async-start(), calls=%async_computation.6 | async-start | bytes 3538944 | tf_op jit(solution)/shard_map/all_gather | solution.py:78
  7.9 14.4 %all-to-all-start = ((s32[32,1,64]{2,1,0:T(1,128)}), s32[32,1,64]{2,1,0:T(1,128)S(1)}, u32[]{:S(2)}, u32[]{:S(2)}) async-start(s32[32,1,64]{2,1,0:T(1,128)} %bitcast.71), calls=%async_computation | async-start | bytes 32768 | tf_op jit(solution)/shard_map/all_to_all | solution.py:92
  63.2 4.8 copy-start.23
  63.2 4.9 copy-start.15
  63.2 4.9 copy-start.24
  63.2 4.9 copy-start.12
  63.2 76.2 %all-to-all-start.1 = ((bf16[32,64,768]{2,1,0:T(8,128)(2,1)}), bf16[32,64,768]{2,1,0:T(8,128)(2,1)}, u32[]{:S(2)}, u32[]{:S(2)}) async-start(bf16[32,64,768]{2,1,0:T(8,128)(2,1)} %bitcast.66), calls=%async_computation.1 | async-start | bytes 6291456 | tf_op jit(solution)/shard_map/all_to_all | solution.py:94
  68.0 311.1 %reduce-scatter.11.cloned.1.call-start = ((), (), s32[]{:S(2)}) async-start(), calls=%async_computation.8 | async-start | bytes 3244032 | tf_op jit(solution)/shard_map/reduce_scatter | solution.py:113
  73.1 3.9 copy-start.14
  73.1 4.2 copy-start.22
  256.0 3.5 copy-start.2
  256.0 3.6 copy-start.3
  256.0 3.6 copy-start.4
  256.0 3.6 copy-start.5
  256.0 3.7 copy-start.6
  256.0 4.1 copy-start.7
  256.0 4.4 copy-start.8
  256.1 4.4 copy-start.16
  256.1 4.4 copy-start.17
  256.1 4.4 copy-start.18
  256.1 4.4 copy-start.19
  256.1 4.4 copy-start.20
  256.1 4.4 copy-start.21
  260.5 8.8 %copy-start.9 = (f32[800,1024]{1,0:T(8,128)S(1)}, f32[800,1024]{1,0:T(8,128)}, u32[]{:S(2)}) copy-start(f32[800,1024]{1,0:T(8,128)} %broadcast_multiply_fusion) | copy-start | bytes 9830404
  260.5 8.8 %copy-start.13 = (f32[32,1024]{1,0:T(8,128)S(1)}, f32[32,1024]{1,0:T(8,128)}, u32[]{:S(2)}) copy-start(f32[32,1024]{1,0:T(8,128)} %fusion.30) | copy-start | bytes 393220
  260.5 8.8 %copy-start.25 = (bf16[768,1024]{1,0:T(8,128)(2,1)S(1)}, bf16[768,1024]{1,0:T(8,128)(2,1)}, u32[]{:S(2)}) copy-start(bf16[768,1024]{1,0:T(8,128)(2,1)} %param.28) | copy-start | bytes 4718596
  277.9 1.3 copy-start.11
  278.0 207.6 %reduce-scatter.9.cloned.1.call-start = ((), (), s32[]{:S(2)}) async-start(), calls=%async_computation.7 | async-start | bytes 3244032 | tf_op jit(solution)/shard_map/reduce_scatter | solution.py:112
  284.3 344.2 %reduce-scatter.15.cloned.1.call-start = ((), (), s32[]{:S(2)}) async-start(), calls=%async_computation.10 | async-start | bytes 4325376
  300.1 467.9 %reduce-scatter.13.cloned.1.call-start = ((), (), s32[]{:S(2)}) async-start(), calls=%async_computation.9 | async-start | bytes 4325376
  309.2 1.7 copy-start.1
  (2 other events, 1.9 us)
Sparse Core Ops, SparseCore 0:
  9.9 35.0 all-gather.1
  278.1 100.9 reduce-scatter.10
  385.0 100.4 reduce-scatter.8
  488.2 140.2 reduce-scatter.14
  631.2 136.7 reduce-scatter.12
where the time goes:
time: 779 us; the launch traced here: 775 us
  waiting for transfers between devices  537 us (69%)
  local copies, waits for them, and re-layouts  155 us (20%)
  matrix products  30.6 us (4%)
  other arithmetic  21.3 us (3%)
  between operations  18.5 us (2%)
  starting transfers between devices  12.2 us (2%)
    unnamed x7, waiting for transfers between devices  283 us
    reduce_scatter x1, waiting for transfers between devices, local(): lax.psum_scatter(grads[0], ('hst', 'dev'), scatter_dimension=0, tiled=True)  107 us
    gather x15, local copies, waits for them, and re-layouts, local_step(): picked = frontier[nbr_rows[:, k]].astype(jnp.float32)  106 us
    reduce_scatter x1, waiting for transfers between devices, local(): lax.psum_scatter(grads[1], ('hst', 'dev'), scatter_dimension=0, tiled=True)  67 us
    all_to_all x1, waiting for transfers between devices, local(): lax.all_to_all(row_data, ('hst', 'dev'), split_axis=0, concat_axis=0, til...  55.9 us
    all_gather x1, waiting for transfers between devices, local(): shard_rows = lax.all_gather(cache_blocks, 'dev', axis=1, tiled=True)  22.6 us
  transfers between devices with their start and end apart: 7, of which 7 were waited for; matrix products, arithmetic and copies ran while one was open for 6% of the time, Pallas kernels for 0%

commit v1 on v0

v1 whole, which is shorter than its diff:
```python
import jax
import jax.numpy as jnp
from jax import lax
from jax.sharding import PartitionSpec as P

CSLOT = 2
BOTH = ("hst", "dev")


def pick_matrix(ids, used, valid, dtype=jnp.bfloat16):
    slots = valid.shape[0]
    slot = lax.broadcasted_iota(jnp.int32, (slots, ids.shape[1]), 0)
    named = jnp.where(used, ids, -1)
    total = jnp.zeros(slot.shape, jnp.float32)
    for k in range(ids.shape[0]):
        total = total + jnp.where(named[k][None, :] == slot, 1.0, 0.0)
    return jnp.where(valid[:, None], total, 0.0).astype(dtype)


def contract(left, right, dim_left, dim_right):
    return lax.dot_general(
        left, right, (((dim_left,), (dim_right,)), ((), ())), preferred_element_type=jnp.float32
    )


def local(
    features,
    cache_blocks,
    plan,
    miss_ids,
    miss_counts,
    self_ids,
    nbr_ids,
    hop_counts,
    seed_counts,
    w_self1,
    w_nbr1,
    w_self2,
    w_nbr2,
    cotangent,
):
    bf16, f32 = jnp.bfloat16, jnp.float32
    home_rows, width_in = features.shape
    slot_count = miss_ids.shape[3]
    n_hst, n_dev = lax.axis_size("hst"), lax.axis_size("dev")
    device_count = n_hst * n_dev
    nodes, fan2 = nbr_ids.shape
    seeds = seed_counts.shape[0]
    fan1 = (nodes - seeds) // seeds
    hidden = w_self1.shape[1]
    part = hidden // device_count
    cache_rows = cache_blocks.shape[1]
    block = cache_rows // CSLOT

    everyones = lax.all_gather(cache_blocks[0], "dev", axis=0, tiled=True)
    requests = lax.all_to_all(
        miss_ids.reshape(device_count, slot_count), BOTH, split_axis=0, concat_axis=0, tiled=True
    ).reshape(-1)
    cot_parts = cotangent.reshape(seeds, n_hst, n_dev, part).transpose(2, 0, 1, 3)
    cot_cols = lax.all_to_all(
        cot_parts.reshape(n_dev, seeds, n_hst * part), "dev", split_axis=0, concat_axis=0, tiled=True
    ).reshape(n_dev * seeds, n_hst * part)

    from_home = features[jnp.minimum(requests, home_rows - 1)]
    blocks = everyones.reshape(-1, block, width_in)
    new_cache = jnp.concatenate(
        [lax.dynamic_index_in_dim(blocks, plan[0, j], 0, keepdims=False) for j in range(CSLOT)], 0
    )
    row = lax.broadcasted_iota(jnp.int32, (cache_rows, requests.shape[0]), 0)
    in_cache = ((requests - home_rows)[None, :] == row).astype(bf16)
    from_cache = contract(in_cache, new_cache, 0, 0).astype(bf16)
    row_data = jnp.where((requests < home_rows)[:, None], from_home, from_cache)
    fetched = lax.all_to_all(
        row_data.reshape(device_count, slot_count, width_in), BOTH, split_axis=0, concat_axis=0, tiled=True
    ).reshape(device_count * slot_count, width_in)

    valid = (
        lax.broadcasted_iota(jnp.int32, (device_count, slot_count), 1)
        < miss_counts.reshape(device_count)[:, None]
    ).reshape(-1)
    hop_used = lax.broadcasted_iota(jnp.int32, (fan2, nodes), 0) < hop_counts[None, :]
    pick_nbr = pick_matrix(nbr_ids.T, hop_used, valid)
    pick_self = pick_matrix(self_ids[None, :], jnp.ones((1, nodes), bool), valid)
    hop_div = hop_counts.astype(f32)[:, None]
    seed_div = seed_counts.astype(f32)[:, None]

    used_two = (jnp.arange(fan1, dtype=jnp.int32)[None, :] < seed_counts[:, None]).astype(f32)
    back_self = contract(cotangent, w_self2, 1, 1)
    back_mean = contract(cotangent, w_nbr2, 1, 1) / seed_div
    back_hop = (back_mean[:, None, :] * used_two[:, :, None]).reshape(seeds * fan1, hidden)
    back_hidden = jnp.concatenate([back_self, back_hop], 0)

    own_rows = contract(pick_self, fetched, 0, 0).astype(bf16)
    mean_one = (contract(pick_nbr, fetched, 0, 0) / hop_div).astype(bf16)
    pre = jnp.dot(own_rows, w_self1, preferred_element_type=f32) + jnp.dot(
        mean_one, w_nbr1, preferred_element_type=f32
    )
    gate = jax.nn.sigmoid(pre)
    hidden_one = (pre * gate).astype(bf16)
    back_pre = (back_hidden * gate * (1.0 + pre * (1.0 - gate))).astype(bf16)

    place = lax.broadcasted_iota(jnp.int32, (seeds, nodes), 1) - seeds
    first = lax.broadcasted_iota(jnp.int32, (seeds, nodes), 0) * fan1
    pick_two = ((place >= first) & (place < first + seed_counts[:, None])).astype(bf16)
    seed_rows = hidden_one[:seeds]
    mean_two = (jnp.dot(pick_two, hidden_one, preferred_element_type=f32) / seed_div).astype(bf16)
    embedding = (
        jnp.dot(seed_rows, w_self2, preferred_element_type=f32)
        + jnp.dot(mean_two, w_nbr2, preferred_element_type=f32)
    ).astype(bf16)

    terms = jnp.concatenate(
        [contract(back_pre, own_rows, 0, 0).astype(bf16), contract(back_pre, mean_one, 0, 0).astype(bf16)], 1
    )
    terms = lax.all_to_all(
        terms.reshape(n_hst, n_dev, part, 2 * width_in), "dev", split_axis=1, concat_axis=1, tiled=True
    )
    sum_one = jnp.sum(terms.astype(f32), 1).astype(bf16)
    rows_two = lax.all_gather(jnp.concatenate([seed_rows, mean_two], 1), "dev", axis=0, tiled=True)
    sum_two = contract(cot_cols, rows_two, 0, 0).astype(bf16).reshape(n_hst, part, 2 * hidden)
    both = lax.all_to_all(
        jnp.concatenate([sum_one, sum_two], 2), "hst", split_axis=0, concat_axis=0, tiled=True
    )
    total = jnp.sum(both.astype(f32), 0)
    cuts = (0, width_in, 2 * width_in, 2 * width_in + hidden, 2 * width_in + 2 * hidden)
    grads = tuple(total[:, a:b].T for a, b in zip(cuts[:-1], cuts[1:]))
    return (embedding, new_cache[None], *grads)


def solution(mesh):
    return jax.shard_map(
        local,
        mesh=mesh,
        in_specs=(
            P(BOTH, None),
            P("hst", "dev", None),
            P("hst", "dev"),
            P(BOTH, None, None, None),
            P(BOTH, None, None),
            P(BOTH),
            P(BOTH, None),
            P(BOTH),
            P(BOTH),
            P(),
            P(),
            P(),
            P(),
            P(BOTH, None),
        ),
        out_specs=(
            P(BOTH, None),
            P("hst", "dev", None),
            P(None, BOTH),
            P(None, BOTH),
            P(None, BOTH),
            P(None, BOTH),
        ),
        check_vma=False,
    )
```

time: 779 us -> 261 us (0.34)
  waiting for transfers between devices: 537 us -> 119 us
  local copies, waits for them, and re-layouts: 155 us -> 34.1 us
  matrix products: 30.6 us -> 49 us
  starting transfers between devices: 12.2 us -> 24.6 us
    unnamed x7 -> x2, waiting for transfers between devices: 283 us -> 0.7 us
    reduce_scatter x2 -> x0, waiting for transfers between devices: 173 us -> none  [the longest x1 107 us: local(): lax.psum_scatter(grads[0], ('hst', 'dev'), scatter_dimension=0, tiled=True)]
    gather x17 -> x1, local copies, waits for them, and re-layouts: 126 us -> 9.43 us  [local(): from_home = features[jnp.minimum(requests, home_rows - 1)]]
    all_gather x1 -> x2, waiting for transfers between devices: 22.6 us -> 45.2 us  [the longest x1 32.4 us: local(): lax.all_gather(jnp.concatenate([seed_rows, mean_two], 1), 'dev', axis=0,...]
    dot_general x11 -> x13, matrix products: 30.6 us -> 49 us  [the longest x8 38.5 us: contract(): lax.dot_general(left, right, (((dim_left,), (dim_right,)), ((), ())), pre...]
    all_to_all x2 -> x5, waiting for transfers between devices: 57.8 us -> 72.8 us  [the longest x1 51.6 us: local(): lax.all_to_all(row_data.reshape(device_count, slot_count, width_in), BOTH...]
    unnamed x56 -> x36, local copies, waits for them, and re-layouts: 15.2 us -> 1.23 us
    all_to_all x2 -> x5, starting transfers between devices: 12 us -> 24.5 us  [the longest x1 7.3 us: local(): lax.all_to_all(miss_ids.reshape(device_count, slot_count), BOTH, split_ax...]
  transfers between devices with their start and end apart: 7 -> 7, of which waited for: 7 -> 6; matrix products, arithmetic and copies ran while one was open for 6% -> 32% of each run, Pallas kernels for 0% -> 0%
where the time goes in v1:
time: 261 us; the launch traced here: 260 us
  waiting for transfers between devices  119 us (46%)
  matrix products  49 us (19%)
  local copies, waits for them, and re-layouts  34.1 us (13%)
  starting transfers between devices  24.6 us (9%)
  between operations  18.3 us (7%)
  other arithmetic  15.1 us (6%)
    all_to_all x1, waiting for transfers between devices, local(): lax.all_to_all(row_data.reshape(device_count, slot_count, width_in), BOTH...  51.6 us
    dot_general x8, matrix products, contract(): lax.dot_general(left, right, (((dim_left,), (dim_right,)), ((), ())), pre...  38.5 us
    all_gather x1, waiting for transfers between devices, local(): lax.all_gather(jnp.concatenate([seed_rows, mean_two], 1), 'dev', axis=0,...  32.4 us
    all_to_all x1, waiting for transfers between devices, local(): lax.all_to_all(jnp.concatenate([sum_one, sum_two], 2), 'hst', split_axis=...  16.1 us
    all_gather x1, waiting for transfers between devices, local(): everyones = lax.all_gather(cache_blocks[0], 'dev', axis=0, tiled=True)  12.8 us
    gather x1, local copies, waits for them, and re-layouts, local(): from_home = features[jnp.minimum(requests, home_rows - 1)]  9.43 us
    all_to_all x1, starting transfers between devices, local(): lax.all_to_all(miss_ids.reshape(device_count, slot_count), BOTH, split_ax...  7.3 us
    mul x2, local copies, waits for them, and re-layouts, local(): back_mean[:, None, :] * used_two[:, :, None]  6.11 us
  transfers between devices with their start and end apart: 7, of which 6 were waited for; matrix products, arithmetic and copies ran while one was open for 32% of the time, Pallas kernels for 0%

profile of v1, /device:TPU:0, one launch (start us, length us, event | category | flops | bytes accessed | tf_op | source)
XLA Modules:
  0.0 259.7 jit_solution(9861599737827370776)
XLA Ops:
  7.9 7.3 %all-to-all-start = ((s32[32,1,64]{2,1,0:T(1,128)}), s32[32,1,64]{2,1,0:T(1,128)S(1)}, u32[]{:S(2)}, u32[]{:S(2)}) async-start(s32[32,1,64]{2,1,0:T(1,128)} %bitcast.58), calls=%async_computation | async-start | bytes 32768 | tf_op jit(solution)/shard_map/all_to_all | solution.py:56
  20.4 1.9 all-to-all-done
  22.7 9.4 %gather_fusion = bf16[2048,768]{1,0:T(8,128)(2,1)} fusion(bf16[2048,768]{1,0:T(8,128)(2,1)S(1)} %copy-done, s32[2048]{0:T(1024)S(1)} %broadcast_clamp_fusion), kind=kCustom, calls=%fused_computation | custom fusion | bytes 6299648 | tf_op jit(solution)/shard_map/gather | solution.py:64
  32.2 12.8 %all-gather.6.cloned.1.call-done = bf16[1,2048,768]{2,1,0:T(8,128)(2,1)} async-done(((bf16[1,256,768]{2,1,0:T(8,128)(2,1)}), bf16[1,2048,768]{2,1,0:T(8,128)(2,1)}) %all-gather.6.cloned.1.call-update) | async-done | bytes 3145744 | tf_op jit(solution)/shard_map/all_gather | solution.py:55
  46.0 4.4 %broadcast_select_fusion = bf16[2048,768]{1,0:T(8,128)(2,1)} fusion(bf16[2048,768]{1,0:T(8,128)(2,1)} %gather_fusion, pred[2048]{0:T(1024)(128)(4,1)S(1)} %lt.81, s32[2048]{0:T(1024)S(1)} %sub.16, bf16[128,768]{1,0:T(8,128)(2,1)S(1)} %get-tuple-element.26, bf16[128,768]{1,0:T(8,128)(2,1)S(1)} %get-tuple-element.25), kind=kOutput, calls=%fused_computation.50 | convolution fusion | flops 809762816 | bytes 6694912 | tf_op jit(solution)/shard_map/dot_general | solution.py:21
  50.5 4.7 %all-to-all-start.1 = ((bf16[32,64,768]{2,1,0:T(8,128)(2,1)}), bf16[32,64,768]{2,1,0:T(8,128)(2,1)}, u32[]{:S(2)}, u32[]{:S(2)}) async-start(bf16[32,64,768]{2,1,0:T(8,128)(2,1)} %bitcast.52), calls=%async_computation.1 | async-start | bytes 6291456 | tf_op jit(solution)/shard_map/all_to_all | solution.py:73
  56.4 2.3 convolution_divide_fusion
  58.7 2.5 mul.40
  61.2 3.6 %mul.41 = f32[800,1024]{1,0:T(8,128)} reshape(f32[32,25,1024]{2,1,0:T(8,128)} %mul.40) | data formatting | bytes 6553600 | tf_op jit(solution)/shard_map/mul | solution.py:90
  68.7 2.3 fusion.48
  71.1 3.9 %broadcast_multiply_fusion = f32[800,1024]{1,0:T(8,128)} fusion(f32[800,1024]{1,0:T(8,128)} %mul.41, f32[800]{0:T(1024)S(1)} %reshape.132), kind=kLoop, calls=%fused_computation.58 | loop fusion | flops 819200 | bytes 6556800 | tf_op jit(solution)/shard_map/mul | solution.py:90
  75.0 51.6 %all-to-all-done.1 = bf16[32,64,768]{2,1,0:T(8,128)(2,1)} async-done(((bf16[32,64,768]{2,1,0:T(8,128)(2,1)}), bf16[32,64,768]{2,1,0:T(8,128)(2,1)}, u32[]{:S(2)}, u32[]{:S(2)}) %all-to-all-start.1) | async-done | bytes 3145760 | tf_op jit(solution)/shard_map/all_to_all | solution.py:73
  126.6 3.5 %all-to-all-start.3 = ((bf16[8,32,128]{2,1,0:T(8,128)(2,1)}), bf16[8,32,128]{2,1,0:T(8,128)(2,1)S(1)}, u32[]{:S(2)}, u32[]{:S(2)}) async-start(bf16[8,32,128]{2,1,0:T(8,128)(2,1)} %reshape.129), calls=%async_computation.3 | async-start | bytes 131072 | tf_op jit(solution)/shard_map/all_to_all | solution.py:60
  130.2 5.3 %fusion.26 = bf16[832,768]{1,0:T(8,128)(2,1)S(1)} fusion(bf16[2048,768]{1,0:T(8,128)(2,1)} %bitcast.8, s32[832]{0:T(1024)S(1)} %copy-done.17, pred[2048]{0:T(1024)(128)(4,1)S(1)} %lt.79), kind=kOutput, calls=%fused_computation.59 | convolution fusion | flops 2624700416 | bytes 4429056 | tf_op jit(solution)/shard_map/dot_general | solution.py:21
  137.0 18.1 %divide_convert_fusion = bf16[832,768]{1,0:T(8,128)(2,1)S(1)} fusion(f32[832]{0:T(1024)S(1)} %convert_element_type.66, bf16[2048,768]{1,0:T(8,128)(2,1)} %bitcast.8, s32[832]{0:T(1024)S(1)} %get-tuple-element.7, s32[832]{0:T(1024)S(1)} %get-tuple-element.8, s32[832]{0:T(1024)S(1)} %get-tuple-element.9, s32[832]{0:T(1024)S(1)} %get-tuple-element.10, ...), kind=kOutput, calls=%fused_computation.51 | convolution fusion | flops 2696904704 | bytes 4478976 | tf_op jit(solution)/shard_map/dot_general | solution.py:21
  155.2 3.9 %fusion.25 = (bf16[832,1024]{1,0:T(8,128)(2,1)S(1)}, bf16[832,1024]{1,0:T(8,128)(2,1)}) fusion(f32[800,1024]{1,0:T(8,128)S(1)} %copy-done.2, f32[32,1024]{1,0:T(8,128)S(1)} %fusion.48, f32[832,1024]{1,0:T(8,128)S(1)} %fusion.47, bf16[832,768]{1,0:T(8,128)(2,1)S(1)} %divide_convert_fusion, bf16[768,1024]{1,0:T(8,128)(2,1)S(1)} %copy-done.16), kind=kOutput, calls=%fused_computation.45 | convolution fusion | flops 1319698432 | bytes 13074432 | tf_op jit(solution)/shard_map/dot_general | solution.py:95
  159.0 1.8 convolution_convert_fusion.2
  160.9 1.8 convolution_convert_fusion.3
  162.7 2.0 pad_maximum_fusion
  164.7 4.7 %copy.25 = bf16[1024,1536]{1,0:T(8,128)(2,1)} copy(bf16[1024,1536]{0,1:T(8,128)(2,1)} %pad_maximum_fusion) | data formatting | bytes 6291456 | tf_op jit(solution)/shard_map/concatenate | solution.py:112
  169.4 3.9 %copy.26 = bf16[4,8,32,1536]{3,2,0,1:T(8,128)(2,1)} copy(bf16[4,8,32,1536]{3,2,1,0:T(8,128)(2,1)} %bitcast.51) | data formatting | bytes 6291456 | tf_op jit(solution)/shard_map/reshape | solution.py:116
  173.3 4.6 %all-to-all-start.2 = ((bf16[4,8,32,1536]{3,2,0,1:T(8,128)(2,1)}), bf16[4,8,32,1536]{3,2,0,1:T(8,128)(2,1)}, u32[]{:S(2)}, u32[]{:S(2)}) async-start(bf16[4,8,32,1536]{3,2,0,1:T(8,128)(2,1)} %copy.26), calls=%async_computation.2 | async-start | bytes 6291456 | tf_op jit(solution)/shard_map/all_to_all | solution.py:115
  178.8 1.9 fusion.27
  182.0 32.4 %all-gather.4.cloned.1.call-done = bf16[256,2048]{1,0:T(8,128)(2,1)} async-done(((bf16[32,2048]{1,0:T(8,128)(2,1)}), bf16[256,2048]{1,0:T(8,128)(2,1)}) %all-gather.4.cloned.1.call-update) | async-done | bytes 1048592 | tf_op jit(solution)/shard_map/all_gather | solution.py:119
  214.4 2.4 convolution_convert_fusion.1
  216.8 3.1 %all-to-all-done.2 = bf16[4,8,32,1536]{3,2,0,1:T(8,128)(2,1)} async-done(((bf16[4,8,32,1536]{3,2,0,1:T(8,128)(2,1)}), bf16[4,8,32,1536]{3,2,0,1:T(8,128)(2,1)}, u32[]{:S(2)}, u32[]{:S(2)}) %all-to-all-start.2) | async-done | bytes 3145760 | tf_op jit(solution)/shard_map/all_to_all | solution.py:115
  220.0 2.4 reduce_sum.21
  222.4 2.0 pad_maximum_fusion.1
  224.4 4.4 %all-to-all-start.4 = ((bf16[4,32,3584]{2,1,0:T(8,128)(2,1)}), bf16[4,32,3584]{2,1,0:T(8,128)(2,1)}, u32[]{:S(2)}, u32[]{:S(2)}) async-start(bf16[4,32,3584]{2,1,0:T(8,128)(2,1)} %pad_maximum_fusion.1), calls=%async_computation.4 | async-start | bytes 1835008 | tf_op jit(solution)/shard_map/all_to_all | solution.py:121
  228.8 1.9 fusion.30
  230.7 2.1 fusion.44
  233.9 16.1 %all-to-all-done.4 = bf16[4,32,3584]{2,1,0:T(8,128)(2,1)} async-done(((bf16[4,32,3584]{2,1,0:T(8,128)(2,1)}), bf16[4,32,3584]{2,1,0:T(8,128)(2,1)}, u32[]{:S(2)}, u32[]{:S(2)}) %all-to-all-start.4) | async-done | bytes 917536 | tf_op jit(solution)/shard_map/all_to_all | solution.py:121
  (70 shorter events, 16.2 us)
Async XLA Ops:
  7.2 15.6 %copy-start = (bf16[2048,768]{1,0:T(8,128)(2,1)S(1)}, bf16[2048,768]{1,0:T(8,128)(2,1)}, u32[]{:S(2)}) copy-start(bf16[2048,768]{1,0:T(8,128)(2,1)} %param.14) | copy-start | bytes 9437188
  7.2 37.8 %all-gather.6.cloned.1.call-start = ((), (), s32[]{:S(2)}) async-start(), calls=%async_computation.6 | async-start | bytes 3538944 | tf_op jit(solution)/shard_map/all_gather | solution.py:55
  7.9 14.4 %all-to-all-start = ((s32[32,1,64]{2,1,0:T(1,128)}), s32[32,1,64]{2,1,0:T(1,128)S(1)}, u32[]{:S(2)}, u32[]{:S(2)}) async-start(s32[32,1,64]{2,1,0:T(1,128)} %bitcast.58), calls=%async_computation | async-start | bytes 32768 | tf_op jit(solution)/shard_map/all_to_all | solution.py:56
  46.0 4.5 %copy-start.3 = (bf16[128,768]{1,0:T(8,128)(2,1)}, bf16[128,768]{1,0:T(8,128)(2,1)S(1)}, u32[]{:S(2)}) copy-start(bf16[128,768]{1,0:T(8,128)(2,1)S(1)} %get-tuple-element.25) | copy-start | bytes 589828
  46.0 4.4 %copy-start.4 = (bf16[128,768]{1,0:T(8,128)(2,1)}, bf16[128,768]{1,0:T(8,128)(2,1)S(1)}, u32[]{:S(2)}) copy-start(bf16[128,768]{1,0:T(8,128)(2,1)S(1)} %get-tuple-element.26) | copy-start | bytes 589828
  50.5 4.7 %copy-start.7 = (bf16[32,1024]{1,0:T(8,128)(2,1)S(1)}, bf16[32,1024]{1,0:T(8,128)(2,1)}, u32[]{:S(2)}) copy-start(bf16[32,1024]{1,0:T(8,128)(2,1)} %param.27) | copy-start | bytes 196612
  50.5 4.9 %copy-start.14 = (s32[32]{0:T(128)S(1)}, s32[32]{0:T(128)}, u32[]{:S(2)}) copy-start(s32[32]{0:T(128)} %param.22) | copy-start | bytes 388
  50.5 76.2 %all-to-all-start.1 = ((bf16[32,64,768]{2,1,0:T(8,128)(2,1)}), bf16[32,64,768]{2,1,0:T(8,128)(2,1)}, u32[]{:S(2)}, u32[]{:S(2)}) async-start(bf16[32,64,768]{2,1,0:T(8,128)(2,1)} %bitcast.52), calls=%async_computation.1 | async-start | bytes 6291456 | tf_op jit(solution)/shard_map/all_to_all | solution.py:73
  55.9 0.5 copy-start.10
  61.2 4.8 %copy-start.9 = (s32[832]{0:T(1024)S(1)}, s32[832]{0:T(1024)}, u32[]{:S(2)}) copy-start(s32[832]{0:T(1024)} %param.21) | copy-start | bytes 9988
  61.2 7.4 %copy-start.8 = (s32[832,15]{0,1:T(8,128)S(1)}, s32[832,15]{0,1:T(8,128)}, u32[]{:S(2)}) copy-start(s32[832,15]{0,1:T(8,128)} %param.20) | copy-start | bytes 149764
  71.1 59.1 %copy-start.17 = (s32[832]{0:T(1024)S(1)}, s32[832]{0:T(1024)}, u32[]{:S(2)}) copy-start(s32[832]{0:T(1024)} %param.19) | copy-start | bytes 9988
  126.6 46.6 %all-to-all-start.3 = ((bf16[8,32,128]{2,1,0:T(8,128)(2,1)}), bf16[8,32,128]{2,1,0:T(8,128)(2,1)S(1)}, u32[]{:S(2)}, u32[]{:S(2)}) async-start(bf16[8,32,128]{2,1,0:T(8,128)(2,1)} %reshape.129), calls=%async_computation.3 | async-start | bytes 131072 | tf_op jit(solution)/shard_map/all_to_all | solution.py:60
  130.2 5.3 %copy-start.15 = (bf16[768,1024]{1,0:T(8,128)(2,1)S(1)}, bf16[768,1024]{1,0:T(8,128)(2,1)}, u32[]{:S(2)}) copy-start(bf16[768,1024]{1,0:T(8,128)(2,1)} %param.23) | copy-start | bytes 4718596
  137.0 18.1 %copy-start.2 = (f32[800,1024]{1,0:T(8,128)S(1)}, f32[800,1024]{1,0:T(8,128)}, u32[]{:S(2)}) copy-start(f32[800,1024]{1,0:T(8,128)} %broadcast_multiply_fusion) | copy-start | bytes 9830404
  137.0 18.1 %copy-start.16 = (bf16[768,1024]{1,0:T(8,128)(2,1)S(1)}, bf16[768,1024]{1,0:T(8,128)(2,1)}, u32[]{:S(2)}) copy-start(bf16[768,1024]{1,0:T(8,128)(2,1)} %param.24) | copy-start | bytes 4718596
  173.3 5.5 %copy-start.11 = (f32[32]{0:T(128)S(1)}, f32[32]{0:T(128)}, u32[]{:S(2)}) copy-start(f32[32]{0:T(128)} %copy-done.10) | copy-start | bytes 388
  173.3 5.5 %copy-start.12 = (s32[32]{0:T(128)S(1)}, s32[32]{0:T(128)}, u32[]{:S(2)}) copy-start(s32[32]{0:T(128)} %get-tuple-element.31) | copy-start | bytes 388
  173.3 5.5 %copy-start.13 = (s32[32]{0:T(128)S(1)}, s32[32]{0:T(128)}, u32[]{:S(2)}) copy-start(s32[32]{0:T(128)} %get-tuple-element.35) | copy-start | bytes 388
  173.3 46.7 %all-to-all-start.2 = ((bf16[4,8,32,1536]{3,2,0,1:T(8,128)(2,1)}), bf16[4,8,32,1536]{3,2,0,1:T(8,128)(2,1)}, u32[]{:S(2)}, u32[]{:S(2)}) async-start(bf16[4,8,32,1536]{3,2,0,1:T(8,128)(2,1)} %copy.26), calls=%async_computation.2 | async-start | bytes 6291456 | tf_op jit(solution)/shard_map/all_to_all | solution.py:115
  177.9 36.6 %all-gather.4.cloned.1.call-start = ((), (), s32[]{:S(2)}) async-start(), calls=%async_computation.5 | async-start | bytes 1179648 | tf_op jit(solution)/shard_map/all_gather | solution.py:119
  180.7 0.6 copy-start.5
  224.4 8.4 %copy-start.6 = (bf16[32,1024]{1,0:T(8,128)(2,1)S(1)}, bf16[32,1024]{1,0:T(8,128)(2,1)}, u32[]{:S(2)}) copy-start(bf16[32,1024]{1,0:T(8,128)(2,1)} %copy-done.5) | copy-start | bytes 196612
  224.4 25.7 %all-to-all-start.4 = ((bf16[4,32,3584]{2,1,0:T(8,128)(2,1)}), bf16[4,32,3584]{2,1,0:T(8,128)(2,1)}, u32[]{:S(2)}, u32[]{:S(2)}) async-start(bf16[4,32,3584]{2,1,0:T(8,128)(2,1)} %pad_maximum_fusion.1), calls=%async_computation.4 | async-start | bytes 1835008 | tf_op jit(solution)/shard_map/all_to_all | solution.py:121
  228.8 4.1 %copy-start.1 = (bf16[1024,1024]{1,0:T(8,128)(2,1)S(1)}, bf16[1024,1024]{1,0:T(8,128)(2,1)}, u32[]{:S(2)}) copy-start(bf16[1024,1024]{1,0:T(8,128)(2,1)} %param.26) | copy-start | bytes 6291460
Sparse Core Ops, SparseCore 0:
  9.9 35.0 all-gather.5
  182.1 32.2 all-gather.3

commit v2 on v1

--- a/solution.py
+++ b/solution.py
@@ -1,6 +1,10 @@
+import functools
+
 import jax
 import jax.numpy as jnp
 from jax import lax
+from jax.experimental import pallas as pl
+from jax.experimental.pallas import tpu as pltpu
 from jax.sharding import PartitionSpec as P
 
 CSLOT = 2
@@ -20,6 +24,181 @@
 def contract(left, right, dim_left, dim_right):
     return lax.dot_general(
         left, right, (((dim_left,), (dim_right,)), ((), ())), preferred_element_type=jnp.float32
+    )
+
+
+def plus(a, b):
+    return a.astype(jnp.float32) + b.astype(jnp.float32)
+
+
+def sum_kernel(n_hst, own_ref, nbr_ref, rows_ref, cot_ref, out_own, out_nbr, out_two,
+               own_c, nbr_c, own_1, nbr_1, own_x, nbr_y, own_2, nbr_2, own_y, nbr_x, own_s, nbr_s,
+               rows_all, two_s, own_z, nbr_z, two_z, send_sem, recv_sem):
+    h, d = lax.axis_index("hst"), lax.axis_index("dev")
+    y, x, c = d // 4, (d // 2) % 2, d % 2
+    to_core = (h, y * 4 + x * 2 + 1 - c)
+    to_x = (h, y * 4 + (1 - x) * 2 + c)
+    to_y = (h, (1 - y) * 4 + x * 2 + c)
+    to_diag = (h, (1 - y) * 4 + (1 - x) * 2 + c)
+    to_hst = [((h + j) % n_hst, d) for j in range(1, n_hst)]
+    peers = [to_core, to_x, to_y, to_diag] + to_hst
+
+    barrier = pltpu.get_barrier_semaphore()
+    for peer in peers:
+        pl.semaphore_signal(barrier, inc=1, device_id=peer, device_id_type=pl.DeviceIdType.MESH)
+    pl.semaphore_wait(barrier, len(peers))
+
+    used = [0]
+
+    def send(src, dst, peer):
+        k = used[0]
+        used[0] = k + 1
+        copy = pltpu.make_async_remote_copy(
+            src_ref=src, dst_ref=dst, send_sem=send_sem.at[k], recv_sem=recv_sem.at[k],
+            device_id=peer, device_id_type=pl.DeviceIdType.MESH,
+        )
+        copy.start()
+        return copy
+
+    own_row = rows_all.at[d]
+    rows_x = send(rows_ref, own_row, to_x)
+    rows_y = send(rows_ref, own_row, to_y)
+    core_own = send(own_ref.at[:, 1 - c], own_c, to_core)
+    rows_diag = send(rows_ref, own_row, to_diag)
+    core_nbr = send(nbr_ref.at[:, 1 - c], nbr_c, to_core)
+    rows_core = [send(rows_ref, own_row, to_core)]
+    rows_all[d] = rows_ref[...]
+
+    part = own_ref.shape[2]
+    bf16 = own_s.dtype
+    count = own_ref.shape[0]
+
+    core_own.wait()
+
+    @pl.loop(0, count)
+    def _(i):
+        own_1[i // 2, i % 2] = plus(own_ref[i, c], own_c[i]).astype(bf16)
+
+    x_own = send(own_1.at[:, 1 - x], own_x, to_x)
+    core_nbr.wait()
+
+    @pl.loop(0, count)
+    def _(i):
+        nbr_1[i // 4, (i // 2) % 2, i % 2] = plus(nbr_ref[i, c], nbr_c[i]).astype(bf16)
+
+    y_nbr = send(nbr_1.at[:, 1 - y], nbr_y, to_y)
+
+    for copy, peer in ((rows_x, to_x), (rows_y, to_y), (rows_diag, to_diag)):
+        copy.wait()
+        slot = rows_all.at[peer[1]]
+        rows_core.append(send(slot, slot, to_core))
+    for copy in rows_core:
+        copy.wait()
+    wide = rows_all.shape[2]
+    gathered = rows_all.shape[0] * rows_all.shape[1]
+    tile = 512
+
+    @pl.loop(0, wide // tile)
+    def _(t):
+        cols = pl.ds(pl.multiple_of(t * tile, tile), tile)
+        block = rows_all[:, :, cols].reshape(gathered, tile)
+        prod = jnp.dot(cot_ref[...], block, preferred_element_type=jnp.float32)
+        two_s[:, :, cols] = prod.astype(bf16).reshape(n_hst, part, tile)
+
+    two_copies = [send(two_s.at[peer[0]], two_z.at[j], peer) for j, peer in enumerate(to_hst)]
+
+    x_own.wait()
+
+    @pl.loop(0, count // 2)
+    def _(i):
+        own_2[i // 2, i % 2] = plus(own_1[i, x], own_x[i]).astype(bf16)
+
+    y_own = send(own_2.at[:, 1 - y], own_y, to_y)
+    y_nbr.wait()
+
+    @pl.loop(0, count // 2)
+    def _(i):
+        nbr_2[i // 2, i % 2] = plus(nbr_1[i // 2, y, i % 2], nbr_y[i // 2, i % 2]).astype(bf16)
+
+    x_nbr = send(nbr_2.at[:, 1 - x], nbr_x, to_x)
+
+    y_own.wait()
+
+    @pl.loop(0, n_hst)
+    def _(i):
+        own_s[i] = plus(own_2[i, y], own_y[i]).astype(bf16)
+
+    own_copies = [send(own_s.at[peer[0]], own_z.at[j], peer) for j, peer in enumerate(to_hst)]
+    x_nbr.wait()
+
+    @pl.loop(0, n_hst)
+    def _(i):
+        nbr_s[i] = plus(nbr_2[i, x], nbr_x[i]).astype(bf16)
+
+    nbr_copies = [send(nbr_s.at[peer[0]], nbr_z.at[j], peer) for j, peer in enumerate(to_hst)]
+
+    for copies, mine, landed, out in (
+        (two_copies, two_s, two_z, out_two),
+        (own_copies, own_s, own_z, out_own),
+        (nbr_copies, nbr_s, nbr_z, out_nbr),
+    ):
+        for copy in copies:
+            copy.wait()
+        total = mine[h].astype(jnp.float32)
+        for j in range(n_hst - 1):
+            total = total + landed[j].astype(jnp.float32)
+        out[...] = total
+
+
+def sum_over_devices(n_hst, terms_own, terms_nbr, rows, cot_rows):
+    hidden, width = terms_own.shape
+    seeds, wide = rows.shape
+    part = hidden // (n_hst * 8)
+    bf16, f32 = jnp.bfloat16, jnp.float32
+    count = n_hst * 4
+    vmem = lambda *shape: pltpu.VMEM(shape, bf16)
+    others = n_hst - 1
+    copies = 13 + 3 * others
+    return pl.pallas_call(
+        functools.partial(sum_kernel, n_hst),
+        out_shape=(
+            jax.ShapeDtypeStruct((part, width), f32),
+            jax.ShapeDtypeStruct((part, width), f32),
+            jax.ShapeDtypeStruct((part, wide), f32),
+        ),
+        in_specs=[pl.BlockSpec(memory_space=pltpu.VMEM)] * 4,
+        out_specs=[pl.BlockSpec(memory_space=pltpu.VMEM)] * 3,
+        scratch_shapes=[
+            vmem(count, part, width),
+            vmem(count, part, width),
+            vmem(count // 2, 2, part, width),
+            vmem(n_hst, 2, 2, part, width),
+            vmem(count // 2, part, width),
+            vmem(n_hst, 2, part, width),
+            vmem(n_hst, 2, part, width),
+            vmem(n_hst, 2, part, width),
+            vmem(n_hst, part, width),
+            vmem(n_hst, part, width),
+            vmem(n_hst, part, width),
+            vmem(n_hst, part, width),
+            vmem(8, seeds, wide),
+            vmem(n_hst, part, wide),
+            vmem(others, part, width),
+            vmem(others, part, width),
+            vmem(others, part, wide),
+            pltpu.SemaphoreType.DMA((copies,)),
+            pltpu.SemaphoreType.DMA((copies,)),
+        ],
+        compiler_params=pltpu.CompilerParams(
+            collective_id=0, has_side_effects=True, vmem_limit_bytes=40 * 1024 * 1024
+        ),
+        cost_estimate=pl.CostEstimate(flops=2 * n_hst * part * 8 * seeds * wide, bytes_accessed=2 * hidden * width * 4, transcendentals=0),
+        name="sum_over_devices",
+    )(
+        terms_own.reshape(count, 2, part, width),
+        terms_nbr.reshape(count, 2, part, width),
+        rows,
+        cot_rows,
     )
 
 
@@ -61,6 +240,7 @@
         cot_parts.reshape(n_dev, seeds, n_hst * part), "dev", split_axis=0, concat_axis=0, tiled=True
     ).reshape(n_dev * seeds, n_hst * part)
 
+    requests, cot_cols = lax.optimization_barrier((requests, cot_cols))
     from_home = features[jnp.minimum(requests, home_rows - 1)]
     blocks = everyones.reshape(-1, block, width_in)
     new_cache = jnp.concatenate(
@@ -81,6 +261,7 @@
     hop_used = lax.broadcasted_iota(jnp.int32, (fan2, nodes), 0) < hop_counts[None, :]
     pick_nbr = pick_matrix(nbr_ids.T, hop_used, valid)
     pick_self = pick_matrix(self_ids[None, :], jnp.ones((1, nodes), bool), valid)
+    pick_nbr, pick_self = lax.optimization_barrier((pick_nbr, pick_self))
     hop_div = hop_counts.astype(f32)[:, None]
     seed_div = seed_counts.astype(f32)[:, None]
 
@@ -109,21 +290,24 @@
         + jnp.dot(mean_two, w_nbr2, preferred_element_type=f32)
     ).astype(bf16)
 
-    terms = jnp.concatenate(
-        [contract(back_pre, own_rows, 0, 0).astype(bf16), contract(back_pre, mean_one, 0, 0).astype(bf16)], 1
-    )
-    terms = lax.all_to_all(
-        terms.reshape(n_hst, n_dev, part, 2 * width_in), "dev", split_axis=1, concat_axis=1, tiled=True
-    )
-    sum_one = jnp.sum(terms.astype(f32), 1).astype(bf16)
-    rows_two = lax.all_gather(jnp.concatenate([seed_rows, mean_two], 1), "dev", axis=0, tiled=True)
-    sum_two = contract(cot_cols, rows_two, 0, 0).astype(bf16).reshape(n_hst, part, 2 * hidden)
-    both = lax.all_to_all(
-        jnp.concatenate([sum_one, sum_two], 2), "hst", split_axis=0, concat_axis=0, tiled=True
-    )
-    total = jnp.sum(both.astype(f32), 0)
-    cuts = (0, width_in, 2 * width_in, 2 * width_in + hidden, 2 * width_in + 2 * hidden)
-    grads = tuple(total[:, a:b].T for a, b in zip(cuts[:-1], cuts[1:]))
+    terms_own = contract(back_pre, own_rows, 0, 0).astype(bf16)
+    terms_nbr = contract(back_pre, mean_one, 0, 0).astype(bf16)
+    rows_two = jnp.concatenate([seed_rows, mean_two], 1)
+    if n_dev == 8:
+        sum_own, sum_nbr, sum_two = sum_over_devices(n_hst, terms_own, terms_nbr, rows_two, cot_cols.T)
+    else:
+        terms = jnp.concatenate([terms_own, terms_nbr], 1).reshape(n_hst, n_dev, part, 2 * width_in)
+        terms = lax.all_to_all(terms, "dev", split_axis=1, concat_axis=1, tiled=True)
+        sum_one = jnp.sum(terms.astype(f32), 1).astype(bf16)
+        rows_all = lax.all_gather(rows_two, "dev", axis=0, tiled=True)
+        sum_two = contract(cot_cols, rows_all, 0, 0).astype(bf16).reshape(n_hst, part, 2 * hidden)
+        both = lax.all_to_all(
+            jnp.concatenate([sum_one, sum_two], 2), "hst", split_axis=0, concat_axis=0, tiled=True
+        )
+        total = jnp.sum(both.astype(f32), 0)
+        sum_own, sum_nbr = total[:, :width_in], total[:, width_in : 2 * width_in]
+        sum_two = total[:, 2 * width_in :]
+    grads = (sum_own.T, sum_nbr.T, sum_two[:, :hidden].T, sum_two[:, hidden:].T)
     return (embedding, new_cache[None], *grads)
 
 

time: 261 us -> 193 us (0.74)
  waiting for transfers between devices: 119 us -> 46 us
  Pallas kernels: 0 us -> 34.6 us
  matrix products: 49 us -> 29.3 us
  starting transfers between devices: 24.6 us -> 15.6 us
  local copies, waits for them, and re-layouts: 34.1 us -> 25.1 us
  other arithmetic: 15.1 us -> 23.9 us
    pallas_call x0 -> x1, Pallas kernels: none -> 34.6 us  [sum_over_devices(): pl.pallas_call(functools.partial(sum_kernel, n_hst), out_shape=(jax.Shape...]
    all_gather x1 -> x0, waiting for transfers between devices: 32.4 us -> none  [local(): lax.all_gather(jnp.concatenate([seed_rows, mean_two], 1), 'dev', axis=0,...]
    all_to_all x2 -> x0, waiting for transfers between devices: 19.3 us -> none  [the longest x1 16.1 us: local(): lax.all_to_all(jnp.concatenate([sum_one, sum_two], 2), 'hst', split_axis=...]
    convert_element_type x0 -> x1, other arithmetic: none -> 17.3 us  [pick_matrix(): return jnp.where(valid[:, None], total, 0.0).astype(dtype)]
    dot_general x8 -> x7, matrix products: 38.5 us -> 22.7 us  [contract(): lax.dot_general(left, right, (((dim_left,), (dim_right,)), ((), ())), pre...]
    all_to_all x1, waiting for transfers between devices: 51.6 us -> 37.8 us  [local(): lax.all_to_all(row_data.reshape(device_count, slot_count, width_in), BOTH...]
    all_to_all x2 -> x0, starting transfers between devices: 8.94 us -> none  [the longest x1 4.59 us: local(): lax.all_to_all(terms.reshape(n_hst, n_dev, part, 2 * width_in), 'dev', sp...]
    all_gather x1, waiting for transfers between devices: 12.8 us -> 4.11 us  [local(): everyones = lax.all_gather(cache_blocks[0], 'dev', axis=0, tiled=True)]
  transfers between devices with their start and end apart: 7 -> 4, of which waited for: 6 -> 3; matrix products, arithmetic and copies ran while one was open for 32% -> 25% of each run, Pallas kernels for 0% -> 0%
where the time goes in v2:
time: 193 us
  waiting for transfers between devices  46 us (24%)
  Pallas kernels  34.6 us (18%)
  matrix products  29.3 us (15%)
  local copies, waits for them, and re-layouts  25.1 us (13%)
  other arithmetic  23.9 us (12%)
  between operations  18.2 us (9%)
  starting transfers between devices  15.6 us (8%)
    all_to_all x1, waiting for transfers between devices, local(): lax.all_to_all(row_data.reshape(device_count, slot_count, width_in), BOTH...  37.8 us
    pallas_call x1, Pallas kernels, sum_over_devices(): pl.pallas_call(functools.partial(sum_kernel, n_hst), out_shape=(jax.Shape...  34.6 us
    dot_general x7, matrix products, contract(): lax.dot_general(left, right, (((dim_left,), (dim_right,)), ((), ())), pre...  22.7 us
    convert_element_type x1, other arithmetic, pick_matrix(): return jnp.where(valid[:, None], total, 0.0).astype(dtype)  17.3 us
    gather x1, local copies, waits for them, and re-layouts, local(): from_home = features[jnp.minimum(requests, home_rows - 1)]  9.37 us
    all_to_all x1, starting transfers between devices, local(): lax.all_to_all(miss_ids.reshape(device_count, slot_count), BOTH, split_ax...  7.3 us
    mul x2, local copies, waits for them, and re-layouts, local(): back_mean[:, None, :] * used_two[:, :, None]  6.07 us
    all_to_all x1, starting transfers between devices, local(): lax.all_to_all(row_data.reshape(device_count, slot_count, width_in), BOTH...  4.9 us
  transfers between devices with their start and end apart: 4, of which 3 were waited for; matrix products, arithmetic and copies ran while one was open for 25% of the time, Pallas kernels for 0%

profile of v2, /device:TPU:0, one launch (start us, length us, event | category | flops | bytes accessed | tf_op | source)
XLA Modules:
  0.0 192.8 jit_solution(7338921355565756126)
XLA Ops:
  7.2 0.7 all-gather.3.cloned.1.call-update
  7.9 7.3 %all-to-all-start = ((s32[32,1,64]{2,1,0:T(1,128)}), s32[32,1,64]{2,1,0:T(1,128)S(1)}, u32[]{:S(2)}, u32[]{:S(2)}) async-start(s32[32,1,64]{2,1,0:T(1,128)} %bitcast.56), calls=%async_computation | async-start | bytes 32768 | tf_op jit(solution)/shard_map/all_to_all | solution.py:235
  15.2 1.8 reshape.92
  17.0 1.1 copy.26
  18.0 0.8 reshape.93
  18.8 3.5 %all-to-all-done = s32[32,1,64]{2,1,0:T(1,128)S(1)} async-done(((s32[32,1,64]{2,1,0:T(1,128)}), s32[32,1,64]{2,1,0:T(1,128)S(1)}, u32[]{:S(2)}, u32[]{:S(2)}) %all-to-all-start) | async-done | bytes 8224 | tf_op jit(solution)/shard_map/all_to_all | solution.py:235
  22.3 3.4 %all-to-all-start.1 = ((bf16[8,32,128]{2,1,0:T(8,128)(2,1)}), bf16[8,32,128]{2,1,0:T(8,128)(2,1)S(1)}, u32[]{:S(2)}, u32[]{:S(2)}) async-start(bf16[8,32,128]{2,1,0:T(8,128)(2,1)} %reshape.93), calls=%async_computation.1 | async-start | bytes 131072 | tf_op jit(solution)/shard_map/all_to_all | solution.py:239
  25.7 1.3 fusion.18
  31.4 0.7 reduce.33
  32.2 9.4 %gather_fusion = bf16[2048,768]{1,0:T(8,128)(2,1)} fusion(bf16[2048,768]{1,0:T(8,128)(2,1)S(1)} %copy-done, s32[2048]{0:T(1024)S(1)} %get-tuple-element.42), kind=kCustom, calls=%fused_computation | custom fusion | bytes 6299648 | tf_op jit(solution)/shard_map/gather | solution.py:244
  41.5 4.1 %all-gather.3.cloned.1.call-done = bf16[1,2048,768]{2,1,0:T(8,128)(2,1)} async-done(((bf16[1,256,768]{2,1,0:T(8,128)(2,1)}), bf16[1,2048,768]{2,1,0:T(8,128)(2,1)}) %all-gather.3.cloned.1.call-update) | async-done | bytes 3145744 | tf_op jit(solution)/shard_map/all_gather | solution.py:234
  45.6 1.0 dynamic-slice_bitcast_fusion.1
  46.7 4.3 %broadcast_select_fusion = bf16[2048,768]{1,0:T(8,128)(2,1)} fusion(bf16[2048,768]{1,0:T(8,128)(2,1)} %gather_fusion, pred[2048]{0:T(1024)(128)(4,1)S(1)} %broadcast_compare_fusion, s32[2048]{0:T(1024)S(1)} %get-tuple-element.41, bf16[128,768]{1,0:T(8,128)(2,1)S(1)} %get-tuple-element.38, bf16[128,768]{1,0:T(8,128)(2,1)S(1)} %get-tuple-element.37), kind=kOutput, calls=%fused_computation.25 | convolution fusion | flops 809762816 | bytes 6694912 | tf_op jit(solution)/shard_map/dot_general | solution.py:25
  51.0 4.9 %all-to-all-start.2 = ((bf16[32,64,768]{2,1,0:T(8,128)(2,1)}), bf16[32,64,768]{2,1,0:T(8,128)(2,1)}, u32[]{:S(2)}, u32[]{:S(2)}) async-start(bf16[32,64,768]{2,1,0:T(8,128)(2,1)} %bitcast.52), calls=%async_computation.2 | async-start | bytes 6291456 | tf_op jit(solution)/shard_map/all_to_all | solution.py:253
  56.4 17.3 %select_convert_fusion = (bf16[2048,832]{1,0:T(8,128)(2,1)}, bf16[2048,832]{1,0:T(8,128)(2,1)}) fusion(s32[832]{0:T(1024)S(1)} %copy-done.11, pred[2048]{0:T(1024)(128)(4,1)S(1)} %lt.65, s32[832]{0:T(1024)S(1)} %get-tuple-element.21, s32[832]{0:T(1024)S(1)} %get-tuple-element.22, s32[832]{0:T(1024)S(1)} %get-tuple-element.23, s32[832]{0:T(1024)S(1)} %get-tuple-element.24, ...), kind=kLoop, calls=%fused_computation.1 | loop fusion | flops 85196800 | bytes 6871040 | tf_op jit(solution)/shard_map/convert_element_type | solution.py:21
  73.8 0.7 convolution_divide_fusion
  74.5 2.5 %mul.40 = f32[32,25,1024]{2,1,0:T(8,128)} broadcast(f32[32,1024]{1,0:T(8,128)S(1)} %convolution_divide_fusion), dimensions={0,2} | broadcast | bytes 3407872 | tf_op jit(solution)/shard_map/mul | solution.py:271
  77.0 3.6 %mul.41 = f32[800,1024]{1,0:T(8,128)} reshape(f32[32,25,1024]{2,1,0:T(8,128)} %mul.40) | data formatting | bytes 6553600 | tf_op jit(solution)/shard_map/mul | solution.py:271
  80.7 3.0 %fusion.20 = f32[32,1024]{1,0:T(8,128)} fusion(bf16[32,1024]{1,0:T(8,128)(2,1)S(1)} %copy-done.7, bf16[1024,1024]{1,0:T(8,128)(2,1)} %param.25), kind=kOutput, calls=%fused_computation.85 | convolution fusion | flops 67108864 | bytes 2293760 | tf_op jit(solution)/shard_map/dot_general | solution.py:25
  83.7 4.0 %broadcast_multiply_fusion = f32[800,1024]{1,0:T(8,128)} fusion(f32[800,1024]{1,0:T(8,128)} %mul.41, f32[800]{0:T(1024)S(1)} %reshape.100), kind=kLoop, calls=%fused_computation.31 | loop fusion | flops 819200 | bytes 6556800 | tf_op jit(solution)/shard_map/mul | solution.py:271
  87.8 1.7 fusion.5
  89.5 37.8 %all-to-all-done.2 = bf16[32,64,768]{2,1,0:T(8,128)(2,1)} async-done(((bf16[32,64,768]{2,1,0:T(8,128)(2,1)}), bf16[32,64,768]{2,1,0:T(8,128)(2,1)}, u32[]{:S(2)}, u32[]{:S(2)}) %all-to-all-start.2) | async-done | bytes 3145760 | tf_op jit(solution)/shard_map/all_to_all | solution.py:253
  127.3 6.0 %convolution_convert_fusion.3 = bf16[832,768]{1,0:T(8,128)(2,1)S(1)} fusion(bf16[2048,832]{1,0:T(8,128)(2,1)} %get-tuple-element.13, bf16[2048,768]{1,0:T(8,128)(2,1)} %bitcast.10), kind=kOutput, calls=%fused_computation.32 | convolution fusion | flops 2617884672 | bytes 7831552 | tf_op jit(solution)/shard_map/dot_general | solution.py:25
  133.3 1.5 fusion.19
  135.3 5.0 %divide_convert_fusion = bf16[832,768]{1,0:T(8,128)(2,1)S(1)} fusion(bf16[2048,832]{1,0:T(8,128)(2,1)S(1)} %copy-done.4, bf16[2048,768]{1,0:T(8,128)(2,1)} %bitcast.10, f32[832]{0:T(1024)S(1)} %convert_element_type.55), kind=kOutput, calls=%fused_computation.26 | convolution fusion | flops 2618523648 | bytes 7834880 | tf_op jit(solution)/shard_map/dot_general | solution.py:25
  140.3 3.2 %fusion.1 = (bf16[832,1024]{1,0:T(8,128)(2,1)S(1)}, bf16[832,1024]{1,0:T(8,128)(2,1)S(1)}) fusion(f32[800,1024]{1,0:T(8,128)S(1)} %copy-done.5, f32[32,1024]{1,0:T(8,128)S(1)} %copy-done.8, f32[832,1024]{1,0:T(8,128)S(1)} %fusion.19, bf16[832,768]{1,0:T(8,128)(2,1)S(1)} %divide_convert_fusion, bf16[768,1024]{1,0:T(8,128)(2,1)S(1)} %copy-done.15), kind=kOutput, calls=%fused_computation.21 | convolution fusion | flops 1319698432 | bytes 13074432 | tf_op jit(solution)/shard_map/dot_general | solution.py:276
  143.5 1.9 convolution_convert_fusion.1
  145.4 1.9 convolution_convert_fusion.2
  148.2 34.6 %sum_over_devices.1 = (f32[32,768]{1,0:T(8,128)S(1)}, f32[32,768]{1,0:T(8,128)S(1)}, f32[32,2048]{1,0:T(8,128)S(1)}) custom-call(bf16[16,2,32,768]{3,2,1,0:T(8,128)(2,1)S(1)} %bitcast.48, bf16[16,2,32,768]{3,2,1,0:T(8,128)(2,1)S(1)} %bitcast.47, bf16[32,2048]{1,0:T(8,128)(2,1)S(1)} %pad_maximum_fusion.2.rows_ref, bf16[128,256]{1,0:T(8,128)(2,1)S(1)} %bitcast.49), custom_call_target="tpu_custom_call" | custom-call | flops 134217728 | bytes 6291456 | tf_op jit(solution)/shard_map/sum_over_devices/pallas_call | solution.py:162
  182.9 0.7 slice_bitcast_fusion
  183.6 1.1 fusion.3
  184.7 0.6 copy.29
  (54 shorter events, 3.5 us)
Async XLA Ops:
  7.2 25.0 %copy-start = (bf16[2048,768]{1,0:T(8,128)(2,1)S(1)}, bf16[2048,768]{1,0:T(8,128)(2,1)}, u32[]{:S(2)}) copy-start(bf16[2048,768]{1,0:T(8,128)(2,1)} %param.14) | copy-start | bytes 9437188
  7.2 38.5 %all-gather.3.cloned.1.call-start = ((), (), s32[]{:S(2)}) async-start(), calls=%async_computation.3 | async-start | bytes 3538944 | tf_op jit(solution)/shard_map/all_gather | solution.py:234
  7.9 14.4 %all-to-all-start = ((s32[32,1,64]{2,1,0:T(1,128)}), s32[32,1,64]{2,1,0:T(1,128)S(1)}, u32[]{:S(2)}, u32[]{:S(2)}) async-start(s32[32,1,64]{2,1,0:T(1,128)} %bitcast.56), calls=%async_computation | async-start | bytes 32768 | tf_op jit(solution)/shard_map/all_to_all | solution.py:235
  22.3 9.8 %all-to-all-start.1 = ((bf16[8,32,128]{2,1,0:T(8,128)(2,1)}), bf16[8,32,128]{2,1,0:T(8,128)(2,1)S(1)}, u32[]{:S(2)}, u32[]{:S(2)}) async-start(bf16[8,32,128]{2,1,0:T(8,128)(2,1)} %reshape.93), calls=%async_computation.1 | async-start | bytes 131072 | tf_op jit(solution)/shard_map/all_to_all | solution.py:239
  46.7 4.3 %copy-start.6 = (bf16[128,768]{1,0:T(8,128)(2,1)}, bf16[128,768]{1,0:T(8,128)(2,1)S(1)}, u32[]{:S(2)}) copy-start(bf16[128,768]{1,0:T(8,128)(2,1)S(1)} %get-tuple-element.38) | copy-start | bytes 589828
  51.0 4.9 %copy-start.12 = (s32[1,4,8]{2,1,0:T(4,128)S(1)}, s32[1,4,8]{2,1,0:T(4,128)}, u32[]{:S(2)}) copy-start(s32[1,4,8]{2,1,0:T(4,128)} %param.18) | copy-start | bytes 388
  51.0 5.2 %copy-start.10 = (s32[832]{0:T(1024)S(1)}, s32[832]{0:T(1024)}, u32[]{:S(2)}) copy-start(s32[832]{0:T(1024)} %param.21) | copy-start | bytes 9988
  51.0 5.2 %copy-start.9 = (s32[832,15]{0,1:T(8,128)S(1)}, s32[832,15]{0,1:T(8,128)}, u32[]{:S(2)}) copy-start(s32[832,15]{0,1:T(8,128)} %param.20) | copy-start | bytes 149764
  51.0 5.4 %copy-start.11 = (s32[832]{0:T(1024)S(1)}, s32[832]{0:T(1024)}, u32[]{:S(2)}) copy-start(s32[832]{0:T(1024)} %param.19) | copy-start | bytes 9988
  51.0 76.2 %all-to-all-start.2 = ((bf16[32,64,768]{2,1,0:T(8,128)(2,1)}), bf16[32,64,768]{2,1,0:T(8,128)(2,1)}, u32[]{:S(2)}, u32[]{:S(2)}) async-start(bf16[32,64,768]{2,1,0:T(8,128)(2,1)} %bitcast.52), calls=%async_computation.2 | async-start | bytes 6291456 | tf_op jit(solution)/shard_map/all_to_all | solution.py:253
  56.4 17.3 %copy-start.13 = (s32[32]{0:T(128)S(1)}, s32[32]{0:T(128)}, u32[]{:S(2)}) copy-start(s32[32]{0:T(128)} %param.22) | copy-start | bytes 388
  56.4 17.3 %copy-start.1 = (bf16[1024,1024]{1,0:T(8,128)(2,1)S(1)}, bf16[1024,1024]{1,0:T(8,128)(2,1)}, u32[]{:S(2)}) copy-start(bf16[1024,1024]{1,0:T(8,128)(2,1)} %param.26) | copy-start | bytes 6291460
  56.4 17.3 %copy-start.7 = (bf16[32,1024]{1,0:T(8,128)(2,1)S(1)}, bf16[32,1024]{1,0:T(8,128)(2,1)}, u32[]{:S(2)}) copy-start(bf16[32,1024]{1,0:T(8,128)(2,1)} %param.27) | copy-start | bytes 196612
  127.3 6.0 %copy-start.14 = (bf16[768,1024]{1,0:T(8,128)(2,1)S(1)}, bf16[768,1024]{1,0:T(8,128)(2,1)}, u32[]{:S(2)}) copy-start(bf16[768,1024]{1,0:T(8,128)(2,1)} %param.23) | copy-start | bytes 4718596
  133.3 2.0 %copy-start.4 = (bf16[2048,832]{1,0:T(8,128)(2,1)S(1)}, bf16[2048,832]{1,0:T(8,128)(2,1)}, u32[]{:S(2)}) copy-start(bf16[2048,832]{1,0:T(8,128)(2,1)} %get-tuple-element.15) | copy-start | bytes 10223620
  135.3 5.0 %copy-start.5 = (f32[800,1024]{1,0:T(8,128)S(1)}, f32[800,1024]{1,0:T(8,128)}, u32[]{:S(2)}) copy-start(f32[800,1024]{1,0:T(8,128)} %broadcast_multiply_fusion) | copy-start | bytes 9830404
  135.3 5.0 %copy-start.8 = (f32[32,1024]{1,0:T(8,128)S(1)}, f32[32,1024]{1,0:T(8,128)}, u32[]{:S(2)}) copy-start(f32[32,1024]{1,0:T(8,128)} %fusion.20) | copy-start | bytes 393220
  135.3 5.0 %copy-start.15 = (bf16[768,1024]{1,0:T(8,128)(2,1)S(1)}, bf16[768,1024]{1,0:T(8,128)(2,1)}, u32[]{:S(2)}) copy-start(bf16[768,1024]{1,0:T(8,128)(2,1)} %param.24) | copy-start | bytes 4718596
  145.4 1.9 copy-start.3
  147.8 35.8 %copy-start.2 = (bf16[1024,1024]{1,0:T(8,128)(2,1)S(1)}, bf16[1024,1024]{1,0:T(8,128)(2,1)}, u32[]{:S(2)}) copy-start(bf16[1024,1024]{1,0:T(8,128)(2,1)} %param.26) | copy-start | bytes 6291460
Sparse Core Ops, SparseCore 0:
  9.9 35.7 all-gather.2

commit v3 on v2

--- a/solution.py
+++ b/solution.py
@@ -200,6 +200,125 @@
         rows,
         cot_rows,
     )
+
+
+def serve_kernel(plan_ref, cache_ref, home_ref, asked_ref, cot_ref, new_ref, rows_ref, cots_ref,
+                 blocks, send_sem, recv_sem):
+    h, d = lax.axis_index("hst"), lax.axis_index("dev")
+    y, x, c = d // 4, (d // 2) % 2, d % 2
+    place = lambda a, b, e: a * 4 + b * 2 + e
+    to_core, to_x, to_y = place(y, x, 1 - c), place(y, 1 - x, c), place(1 - y, x, c)
+    to_diag = place(1 - y, 1 - x, c)
+    peers = [(d + j) % 8 for j in range(1, 8)]
+
+    barrier = pltpu.get_barrier_semaphore()
+    for peer in peers:
+        pl.semaphore_signal(barrier, inc=1, device_id=(h, peer), device_id_type=pl.DeviceIdType.MESH)
+    pl.semaphore_wait(barrier, len(peers))
+
+    used = [0]
+
+    def send(src, dst, peer):
+        k = used[0]
+        used[0] = k + 1
+        copy = pltpu.make_async_remote_copy(
+            src_ref=src, dst_ref=dst, send_sem=send_sem.at[k], recv_sem=recv_sem.at[k],
+            device_id=(h, peer), device_id_type=pl.DeviceIdType.MESH,
+        )
+        copy.start()
+        return copy
+
+    def pass_on(owner, j, peer):
+        slot = blocks.at[owner * CSLOT + j]
+        return send(slot, slot, peer)
+
+    own = lambda j, peer: send(cache_ref.at[j], blocks.at[d * CSLOT + j], peer)
+    x_first, y_last = own(0, to_x), own(1, to_y)
+    x_last, y_first = own(1, to_x), own(0, to_y)
+    core = [own(0, to_core), own(1, to_core)]
+    cots = [send(cot_ref.at[peer], cots_ref.at[d], peer) for peer in peers]
+    for j in range(CSLOT):
+        blocks[d * CSLOT + j] = cache_ref[j]
+    cots_ref[d] = cot_ref[d]
+
+    home_rows = home_ref.shape[0]
+    asked_rows = asked_ref.shape[0]
+    tile = 256
+    tiles = asked_rows // tile
+    bf16 = rows_ref.dtype
+
+    def one_hot(rows, first, count):
+        at = lax.broadcasted_iota(jnp.int32, (tile, count), 1) + first
+        return jnp.where(asked_ref[rows, :] == at, 1.0, 0.0).astype(bf16)
+
+    def from_home(t):
+        rows = pl.ds(pl.multiple_of(t * tile, tile), tile)
+        picked = jnp.dot(one_hot(rows, 0, home_rows), home_ref[...], preferred_element_type=jnp.float32)
+        rows_ref[rows, :] = picked.astype(bf16)
+
+    pl.loop(0, tiles // 2)(from_home)
+
+    x_first.wait()
+    diag_first = pass_on(to_x, 0, to_y)
+    y_last.wait()
+    diag_last = pass_on(to_y, 1, to_x)
+    core += [pass_on(to_x, 0, to_core), pass_on(to_y, 1, to_core)]
+    x_last.wait()
+    core.append(pass_on(to_x, 1, to_core))
+    y_first.wait()
+    core.append(pass_on(to_y, 0, to_core))
+
+    pl.loop(tiles // 2, tiles)(from_home)
+
+    diag_first.wait()
+    core.append(pass_on(to_diag, 0, to_core))
+    diag_last.wait()
+    core.append(pass_on(to_diag, 1, to_core))
+    for copy in core + cots:
+        copy.wait()
+
+    block = cache_ref.shape[1]
+    for j in range(CSLOT):
+        new_ref[pl.ds(j * block, block), :] = blocks[plan_ref[0, j]]
+
+    @pl.loop(0, tiles)
+    def _(t):
+        rows = pl.ds(pl.multiple_of(t * tile, tile), tile)
+        hot = one_hot(rows, home_rows, CSLOT * block)
+        picked = jnp.dot(hot, new_ref[...], preferred_element_type=jnp.float32)
+        rows_ref[rows, :] = (rows_ref[rows, :].astype(jnp.float32) + picked).astype(bf16)
+
+
+def serve_rows(plan, cache, home, asked, cot_parts):
+    _, block, width = cache.shape
+    bf16 = jnp.bfloat16
+    asks = asked.shape[0]
+    vmem = pl.BlockSpec(memory_space=pltpu.VMEM)
+    copies = 21
+    return pl.pallas_call(
+        serve_kernel,
+        out_shape=(
+            jax.ShapeDtypeStruct((CSLOT * block, width), bf16),
+            jax.ShapeDtypeStruct((asks, width), bf16),
+            jax.ShapeDtypeStruct(cot_parts.shape, bf16),
+        ),
+        in_specs=[pl.BlockSpec(memory_space=pltpu.SMEM)] + [vmem] * 4,
+        out_specs=[vmem] * 3,
+        scratch_shapes=[
+            pltpu.VMEM((8 * CSLOT, block, width), bf16),
+            pltpu.SemaphoreType.DMA((copies,)),
+            pltpu.SemaphoreType.DMA((copies,)),
+        ],
+        compiler_params=pltpu.CompilerParams(
+            collective_id=1, has_side_effects=True, vmem_limit_bytes=40 * 1024 * 1024
+        ),
+        cost_estimate=pl.CostEstimate(
+            flops=2 * asks * (home.shape[0] + CSLOT * block) * width,
+            bytes_accessed=4 * (asks + home.shape[0]) * width,
+            transcendentals=0,
+        ),
+        name="serve_rows",
+    )(plan, cache, home, asked, cot_parts)
 
 
 def local(
@@ -231,25 +350,30 @@
     cache_rows = cache_blocks.shape[1]
     block = cache_rows // CSLOT
 
-    everyones = lax.all_gather(cache_blocks[0], "dev", axis=0, tiled=True)
     requests = lax.all_to_all(
         miss_ids.reshape(device_count, slot_count), BOTH, split_axis=0, concat_axis=0, tiled=True
     ).reshape(-1)
     cot_parts = cotangent.reshape(seeds, n_hst, n_dev, part).transpose(2, 0, 1, 3)
-    cot_cols = lax.all_to_all(
-        cot_parts.reshape(n_dev, seeds, n_hst * part), "dev", split_axis=0, concat_axis=0, tiled=True
-    ).reshape(n_dev * seeds, n_hst * part)
-
-    requests, cot_cols = lax.optimization_barrier((requests, cot_cols))
-    from_home = features[jnp.minimum(requests, home_rows - 1)]
-    blocks = everyones.reshape(-1, block, width_in)
-    new_cache = jnp.concatenate(
-        [lax.dynamic_index_in_dim(blocks, plan[0, j], 0, keepdims=False) for j in range(CSLOT)], 0
-    )
-    row = lax.broadcasted_iota(jnp.int32, (cache_rows, requests.shape[0]), 0)
-    in_cache = ((requests - home_rows)[None, :] == row).astype(bf16)
-    from_cache = contract(in_cache, new_cache, 0, 0).astype(bf16)
-    row_data = jnp.where((requests < home_rows)[:, None], from_home, from_cache)
+    cot_parts = cot_parts.reshape(n_dev, seeds, n_hst * part)
+    if n_dev == 8:
+        new_cache, row_data, cot_cols = serve_rows(
+            plan, cache_blocks.reshape(CSLOT, block, width_in), features, requests[:, None], cot_parts
+        )
+        cot_cols = cot_cols.reshape(n_dev * seeds, n_hst * part)
+    else:
+        everyones = lax.all_gather(cache_blocks[0], "dev", axis=0, tiled=True)
+        cot_cols = lax.all_to_all(
+            cot_parts, "dev", split_axis=0, concat_axis=0, tiled=True
+        ).reshape(n_dev * seeds, n_hst * part)
+        from_home = features[jnp.minimum(requests, home_rows - 1)]
+        blocks = everyones.reshape(-1, block, width_in)
+        new_cache = jnp.concatenate(
+            [lax.dynamic_index_in_dim(blocks, plan[0, j], 0, keepdims=False) for j in range(CSLOT)], 0
+        )
+        row = lax.broadcasted_iota(jnp.int32, (cache_rows, requests.shape[0]), 0)
+        in_cache = ((requests - home_rows)[None, :] == row).astype(bf16)
+        from_cache = contract(in_cache, new_cache, 0, 0).astype(bf16)
+        row_data = jnp.where((requests < home_rows)[:, None], from_home, from_cache)
     fetched = lax.all_to_all(
         row_data.reshape(device_count, slot_count, width_in), BOTH, split_axis=0, concat_axis=0, tiled=True
     ).reshape(device_count * slot_count, width_in)
@@ -261,7 +385,7 @@
     hop_used = lax.broadcasted_iota(jnp.int32, (fan2, nodes), 0) < hop_counts[None, :]
     pick_nbr = pick_matrix(nbr_ids.T, hop_used, valid)
     pick_self = pick_matrix(self_ids[None, :], jnp.ones((1, nodes), bool), valid)
-    pick_nbr, pick_self = lax.optimization_barrier((pick_nbr, pick_self))
+    pick_nbr, pick_self = lax.optimization_barrier((pick_nbr.T, pick_self.T))
     hop_div = hop_counts.astype(f32)[:, None]
     seed_div = seed_counts.astype(f32)[:, None]
 
@@ -271,8 +395,8 @@
     back_hop = (back_mean[:, None, :] * used_two[:, :, None]).reshape(seeds * fan1, hidden)
     back_hidden = jnp.concatenate([back_self, back_hop], 0)
 
-    own_rows = contract(pick_self, fetched, 0, 0).astype(bf16)
-    mean_one = (contract(pick_nbr, fetched, 0, 0) / hop_div).astype(bf16)
+    own_rows = contract(pick_self, fetched, 1, 0).astype(bf16)
+    mean_one = (contract(pick_nbr, fetched, 1, 0) / hop_div).astype(bf16)
     pre = jnp.dot(own_rows, w_self1, preferred_element_type=f32) + jnp.dot(
         mean_one, w_nbr1, preferred_element_type=f32
     )

time: 193 us -> 180 us (0.933)
  Pallas kernels: 34.6 us -> 55.9 us
  between operations: 18.2 us -> 0.96 us
  matrix products: 29.3 us -> 22.5 us
  local copies, waits for them, and re-layouts: 25.1 us -> 20 us
  starting transfers between devices: 15.6 us -> 11.2 us
    pallas_call x0 -> x1, Pallas kernels: none -> 21.2 us  [serve_rows(): pl.pallas_call(serve_kernel, out_shape=(jax.ShapeDtypeStruct((CSLOT * blo...]
    gather x1 -> x0, local copies, waits for them, and re-layouts: 9.37 us -> none  [local(): from_home = features[jnp.minimum(requests, home_rows - 1)]]
    unnamed x34 -> x43, local copies, waits for them, and re-layouts: 1.9 us -> 9.17 us
    dot_general x7 -> x6, matrix products: 22.7 us -> 15.8 us  [contract(): lax.dot_general(left, right, (((dim_left,), (dim_right,)), ((), ())), pre...]
    all_gather x1 -> x0, waiting for transfers between devices: 4.11 us -> none  [local(): everyones = lax.all_gather(cache_blocks[0], 'dev', axis=0, tiled=True)]
    all_to_all x1, waiting for transfers between devices: 37.8 us -> 41.6 us  [local(): lax.all_to_all(row_data.reshape(device_count, slot_count, width_in), BOTH...]
    all_to_all x1 -> x0, starting transfers between devices: 3.35 us -> none  [local(): lax.all_to_all(cot_parts.reshape(n_dev, seeds, n_hst * part), 'dev', spli...]
  transfers between devices with their start and end apart: 4 -> 2, of which waited for: 3 -> 2; matrix products, arithmetic and copies ran while one was open for 25% -> 18% of each run, Pallas kernels for 0% -> 0%
where the time goes in v3:
time: 180 us; the launch traced here: 179 us
  Pallas kernels  55.9 us (31%)
  waiting for transfers between devices  46.7 us (26%)
  matrix products  22.5 us (12%)
  other arithmetic  22.2 us (12%)
  local copies, waits for them, and re-layouts  20 us (11%)
  starting transfers between devices  11.2 us (6%)
    all_to_all x1, waiting for transfers between devices, local(): lax.all_to_all(row_data.reshape(device_count, slot_count, width_in), BOTH...  41.6 us
    pallas_call x1, Pallas kernels, sum_over_devices(): pl.pallas_call(functools.partial(sum_kernel, n_hst), out_shape=(jax.Shape...  34.6 us
    pallas_call x1, Pallas kernels, serve_rows(): pl.pallas_call(serve_kernel, out_shape=(jax.ShapeDtypeStruct((CSLOT * blo...  21.2 us
    convert_element_type x1, other arithmetic, pick_matrix(): return jnp.where(valid[:, None], total, 0.0).astype(dtype)  17.3 us
    dot_general x6, matrix products, contract(): lax.dot_general(left, right, (((dim_left,), (dim_right,)), ((), ())), pre...  15.8 us
    unnamed x43, local copies, waits for them, and re-layouts  9.17 us
    all_to_all x1, starting transfers between devices, local(): lax.all_to_all(miss_ids.reshape(device_count, slot_count), BOTH, split_ax...  7.3 us
    mul x2, local copies, waits for them, and re-layouts, local(): back_mean[:, None, :] * used_two[:, :, None]  6.11 us
  transfers between devices with their start and end apart: 2, of which 2 were waited for; matrix products, arithmetic and copies ran while one was open for 18% of the time, Pallas kernels for 0%

profile of v3, /device:TPU:0, one launch (start us, length us, event | category | flops | bytes accessed | tf_op | source)
XLA Modules:
  0.0 179.4 jit_solution(9600631383478117108)
XLA Ops:
  0.6 7.3 %all-to-all-start = ((s32[32,1,64]{2,1,0:T(1,128)}), s32[32,1,64]{2,1,0:T(1,128)S(1)}, u32[]{:S(2)}, u32[]{:S(2)}) async-start(s32[32,1,64]{2,1,0:T(1,128)} %bitcast.50), calls=%async_computation | async-start | bytes 32768 | tf_op jit(solution)/shard_map/all_to_all | solution.py:353
  8.0 1.1 reshape.87
  9.1 0.8 reshape.88.cot_ref
  9.9 5.1 %all-to-all-done = s32[32,1,64]{2,1,0:T(1,128)S(1)} async-done(((s32[32,1,64]{2,1,0:T(1,128)}), s32[32,1,64]{2,1,0:T(1,128)S(1)}, u32[]{:S(2)}, u32[]{:S(2)}) %all-to-all-start) | async-done | bytes 8224 | tf_op jit(solution)/shard_map/all_to_all | solution.py:353
  15.5 0.7 reduce.33
  16.2 1.0 broadcast_in_dim_reshape.3.asked_ref
  17.3 0.8 copy-done.2
  18.1 1.9 %copy-done.5 = bf16[2048,768]{1,0:T(8,128)(2,1)S(1)} copy-done((bf16[2048,768]{1,0:T(8,128)(2,1)S(1)}, bf16[2048,768]{1,0:T(8,128)(2,1)}, u32[]{:S(2)}) %copy-start.5) | copy-done | bytes 3145752
  20.0 1.0 copy-done.6
  21.0 0.7 copy-done.7
  21.6 21.2 %serve_rows.1 = (bf16[256,768]{1,0:T(8,128)(2,1)S(1)}, bf16[2048,768]{1,0:T(8,128)(2,1)S(1)}, bf16[8,32,128]{2,1,0:T(8,128)(2,1)S(1)}) custom-call(s32[1,2]{1,0:T(1,128)S(1)} %copy-done.7, bf16[2,128,768]{2,1,0:T(8,128)(2,1)S(1)} %bitcast.48, bf16[2048,768]{1,0:T(8,128)(2,1)S(1)} %copy-done.5, s32[2048,1]{1,0:T(8,128)S(1)} %broadcast_in_dim_reshape.3.asked_ref, ...), custom_call_target="tpu_custom_call" | custom-call | flops 7247757312 | bytes 12582912 | tf_op jit(solution)/shard_map/serve_rows/pallas_call | solution.py:298
  42.9 1.6 copy-done.1
  45.1 3.9 %all-to-all-start.1 = ((bf16[32,64,768]{2,1,0:T(8,128)(2,1)}), bf16[32,64,768]{2,1,0:T(8,128)(2,1)}, u32[]{:S(2)}, u32[]{:S(2)}) async-start(bf16[32,64,768]{2,1,0:T(8,128)(2,1)} %bitcast.40), calls=%async_computation.1 | async-start | bytes 6291456 | tf_op jit(solution)/shard_map/all_to_all | solution.py:377
  49.5 17.3 %select_convert_fusion = (bf16[832,2048]{1,0:T(8,128)(2,1)}, bf16[832,2048]{1,0:T(8,128)(2,1)}) fusion(s32[832]{0:T(1024)S(1)} %copy-done.15, pred[2048]{0:T(1024)(128)(4,1)S(1)} %lt.49, s32[832]{0:T(1024)S(1)} %get-tuple-element.23, s32[832]{0:T(1024)S(1)} %get-tuple-element.24, s32[832]{0:T(1024)S(1)} %get-tuple-element.25, s32[832]{0:T(1024)S(1)} %get-tuple-element.26, ...), kind=kLoop, calls=%fused_computation | loop fusion | flops 85196800 | bytes 6871040 | tf_op jit(solution)/shard_map/convert_element_type | solution.py:21
  66.8 0.7 convolution_divide_fusion
  67.5 2.5 %mul.40 = f32[32,25,1024]{2,1,0:T(8,128)} broadcast(f32[32,1024]{1,0:T(8,128)S(1)} %convolution_divide_fusion), dimensions={0,2} | broadcast | bytes 3407872 | tf_op jit(solution)/shard_map/mul | solution.py:395
  70.0 3.6 %mul.41 = f32[800,1024]{1,0:T(8,128)} reshape(f32[32,25,1024]{2,1,0:T(8,128)} %mul.40) | data formatting | bytes 6553600 | tf_op jit(solution)/shard_map/mul | solution.py:395
  73.8 0.7 fusion.15
  74.6 4.0 %broadcast_multiply_fusion = f32[800,1024]{1,0:T(8,128)} fusion(f32[800,1024]{1,0:T(8,128)} %mul.41, f32[800]{0:T(1024)S(1)} %reshape.94), kind=kLoop, calls=%fused_computation.27 | loop fusion | flops 819200 | bytes 6556800 | tf_op jit(solution)/shard_map/mul | solution.py:395
  78.7 41.6 %all-to-all-done.1 = bf16[32,64,768]{2,1,0:T(8,128)(2,1)} async-done(((bf16[32,64,768]{2,1,0:T(8,128)(2,1)}), bf16[32,64,768]{2,1,0:T(8,128)(2,1)}, u32[]{:S(2)}, u32[]{:S(2)}) %all-to-all-start.1) | async-done | bytes 3145760 | tf_op jit(solution)/shard_map/all_to_all | solution.py:377
  120.4 5.8 %convolution_convert_fusion.2 = bf16[832,768]{1,0:T(8,128)(2,1)S(1)} fusion(bf16[832,2048]{1,0:T(8,128)(2,1)} %get-tuple-element.14, bf16[2048,768]{1,0:T(8,128)(2,1)} %bitcast.5), kind=kOutput, calls=%fused_computation.28 | convolution fusion | flops 2617884672 | bytes 7831552 | tf_op jit(solution)/shard_map/dot_general | solution.py:25
  126.2 1.5 fusion.14
  128.2 4.9 %divide_convert_fusion = bf16[832,768]{1,0:T(8,128)(2,1)S(1)} fusion(bf16[832,2048]{1,0:T(8,128)(2,1)S(1)} %copy-done.10, bf16[2048,768]{1,0:T(8,128)(2,1)} %bitcast.5, f32[832]{0:T(1024)S(1)} %convert_element_type.52), kind=kOutput, calls=%fused_computation.23 | convolution fusion | flops 2618523648 | bytes 7834880 | tf_op jit(solution)/shard_map/dot_general | solution.py:25
  133.1 3.1 %fusion.1 = (bf16[832,1024]{1,0:T(8,128)(2,1)S(1)}, bf16[832,1024]{1,0:T(8,128)(2,1)S(1)}) fusion(f32[800,1024]{1,0:T(8,128)S(1)} %copy-done.11, f32[32,1024]{1,0:T(8,128)S(1)} %fusion.15, f32[832,1024]{1,0:T(8,128)S(1)} %fusion.14, bf16[832,768]{1,0:T(8,128)(2,1)S(1)} %divide_convert_fusion, bf16[768,1024]{1,0:T(8,128)(2,1)S(1)} %copy-done.19), kind=kOutput, calls=%fused_computation.20 | convolution fusion | flops 1319698432 | bytes 13074432 | tf_op jit(solution)/shard_map/dot_general | solution.py:400
  136.2 1.9 %convolution_convert_fusion = bf16[1024,768]{1,0:T(8,128)(2,1)S(1)} fusion(bf16[832,1024]{1,0:T(8,128)(2,1)S(1)} %get-tuple-element.37, bf16[832,768]{1,0:T(8,128)(2,1)S(1)} %divide_convert_fusion), kind=kOutput, calls=%fused_computation.25 | convolution fusion | flops 1309409280 | bytes 4554752 | tf_op jit(solution)/shard_map/dot_general | solution.py:25
  138.1 1.9 %convolution_convert_fusion.1 = bf16[1024,768]{1,0:T(8,128)(2,1)S(1)} fusion(bf16[832,1024]{1,0:T(8,128)(2,1)S(1)} %get-tuple-element.37, bf16[832,768]{1,0:T(8,128)(2,1)S(1)} %convolution_convert_fusion.2), kind=kOutput, calls=%fused_computation.26 | convolution fusion | flops 1309409280 | bytes 4554752 | tf_op jit(solution)/shard_map/dot_general | solution.py:25
  140.9 34.6 %sum_over_devices.1 = (f32[32,768]{1,0:T(8,128)S(1)}, f32[32,768]{1,0:T(8,128)S(1)}, f32[32,2048]{1,0:T(8,128)S(1)}) custom-call(bf16[16,2,32,768]{3,2,1,0:T(8,128)(2,1)S(1)} %bitcast.42, bf16[16,2,32,768]{3,2,1,0:T(8,128)(2,1)S(1)} %bitcast.41, bf16[32,2048]{1,0:T(8,128)(2,1)S(1)} %pad_maximum_fusion.rows_ref, bf16[128,256]{1,0:T(8,128)(2,1)S(1)} %bitcast.44), custom_call_target="tpu_custom_call" | custom-call | flops 134217728 | bytes 6291456 | tf_op jit(solution)/shard_map/sum_over_devices/pallas_call | solution.py:162
  175.5 0.7 slice_bitcast_fusion
  176.2 1.1 fusion.3
  177.3 0.7 copy.33
  178.1 0.6 copy.34
  178.7 0.6 copy.35
  (52 shorter events, 3.4 us)
Async XLA Ops:
  0.6 73.2 %copy-start = (bf16[1024,1024]{1,0:T(8,128)(2,1)S(1)}, bf16[1024,1024]{1,0:T(8,128)(2,1)}, u32[]{:S(2)}) copy-start(bf16[1024,1024]{1,0:T(8,128)(2,1)} %param.25) | copy-start | bytes 6291460
  0.6 14.4 %all-to-all-start = ((s32[32,1,64]{2,1,0:T(1,128)}), s32[32,1,64]{2,1,0:T(1,128)S(1)}, u32[]{:S(2)}, u32[]{:S(2)}) async-start(s32[32,1,64]{2,1,0:T(1,128)} %bitcast.50), calls=%async_computation | async-start | bytes 32768 | tf_op jit(solution)/shard_map/all_to_all | solution.py:353
  17.2 0.8 copy-start.2
  18.1 1.9 %copy-start.5 = (bf16[2048,768]{1,0:T(8,128)(2,1)S(1)}, bf16[2048,768]{1,0:T(8,128)(2,1)}, u32[]{:S(2)}) copy-start(bf16[2048,768]{1,0:T(8,128)(2,1)} %home_ref.1) | copy-start | bytes 9437188
  20.0 1.0 copy-start.6
  21.0 0.7 copy-start.7
  42.9 1.6 copy-start.1
  44.5 0.6 copy-start.3
  45.1 3.9 %copy-start.16 = (s32[1,4,8]{2,1,0:T(4,128)S(1)}, s32[1,4,8]{2,1,0:T(4,128)}, u32[]{:S(2)}) copy-start(s32[1,4,8]{2,1,0:T(4,128)} %param.18) | copy-start | bytes 388
  45.1 4.1 %copy-start.14 = (s32[832]{0:T(1024)S(1)}, s32[832]{0:T(1024)}, u32[]{:S(2)}) copy-start(s32[832]{0:T(1024)} %param.21) | copy-start | bytes 9988
  45.1 4.1 %copy-start.13 = (s32[832,15]{0,1:T(8,128)S(1)}, s32[832,15]{0,1:T(8,128)}, u32[]{:S(2)}) copy-start(s32[832,15]{0,1:T(8,128)} %param.20) | copy-start | bytes 149764
  45.1 4.3 %copy-start.15 = (s32[832]{0:T(1024)S(1)}, s32[832]{0:T(1024)}, u32[]{:S(2)}) copy-start(s32[832]{0:T(1024)} %param.19) | copy-start | bytes 9988
  45.1 75.2 %all-to-all-start.1 = ((bf16[32,64,768]{2,1,0:T(8,128)(2,1)}), bf16[32,64,768]{2,1,0:T(8,128)(2,1)}, u32[]{:S(2)}, u32[]{:S(2)}) async-start(bf16[32,64,768]{2,1,0:T(8,128)(2,1)} %bitcast.40), calls=%async_computation.1 | async-start | bytes 6291456 | tf_op jit(solution)/shard_map/all_to_all | solution.py:377
  49.5 17.3 %copy-start.17 = (s32[32]{0:T(128)S(1)}, s32[32]{0:T(128)}, u32[]{:S(2)}) copy-start(s32[32]{0:T(128)} %param.22) | copy-start | bytes 388
  49.5 17.3 %copy-start.8 = (bf16[1024,1024]{1,0:T(8,128)(2,1)S(1)}, bf16[1024,1024]{1,0:T(8,128)(2,1)}, u32[]{:S(2)}) copy-start(bf16[1024,1024]{1,0:T(8,128)(2,1)} %param.26) | copy-start | bytes 6291460
  49.5 17.3 %copy-start.12 = (bf16[32,1024]{1,0:T(8,128)(2,1)S(1)}, bf16[32,1024]{1,0:T(8,128)(2,1)}, u32[]{:S(2)}) copy-start(bf16[32,1024]{1,0:T(8,128)(2,1)} %param.27) | copy-start | bytes 196612
  74.6 4.0 %copy-start.4 = (bf16[8,32,128]{2,1,0:T(8,128)(2,1)S(1)}, bf16[8,32,128]{2,1,0:T(8,128)(2,1)}, u32[]{:S(2)}) copy-start(bf16[8,32,128]{2,1,0:T(8,128)(2,1)} %copy-done.3) | copy-start | bytes 196612
  120.4 5.8 %copy-start.18 = (bf16[768,1024]{1,0:T(8,128)(2,1)S(1)}, bf16[768,1024]{1,0:T(8,128)(2,1)}, u32[]{:S(2)}) copy-start(bf16[768,1024]{1,0:T(8,128)(2,1)} %param.23) | copy-start | bytes 4718596
  126.2 2.0 %copy-start.10 = (bf16[832,2048]{1,0:T(8,128)(2,1)S(1)}, bf16[832,2048]{1,0:T(8,128)(2,1)}, u32[]{:S(2)}) copy-start(bf16[832,2048]{1,0:T(8,128)(2,1)} %get-tuple-element.16) | copy-start | bytes 10223620
  128.2 4.9 %copy-start.11 = (f32[800,1024]{1,0:T(8,128)S(1)}, f32[800,1024]{1,0:T(8,128)}, u32[]{:S(2)}) copy-start(f32[800,1024]{1,0:T(8,128)} %broadcast_multiply_fusion) | copy-start | bytes 9830404
  128.2 4.9 %copy-start.19 = (bf16[768,1024]{1,0:T(8,128)(2,1)S(1)}, bf16[768,1024]{1,0:T(8,128)(2,1)}, u32[]{:S(2)}) copy-start(bf16[768,1024]{1,0:T(8,128)(2,1)} %param.24) | copy-start | bytes 4718596
  140.4 35.8 %copy-start.9 = (bf16[1024,1024]{1,0:T(8,128)(2,1)S(1)}, bf16[1024,1024]{1,0:T(8,128)(2,1)}, u32[]{:S(2)}) copy-start(bf16[1024,1024]{1,0:T(8,128)(2,1)} %param.26) | copy-start | bytes 6291460

commit v4 on v3

--- a/solution.py
+++ b/solution.py
@@ -202,28 +202,34 @@
     )
 
 
-def serve_kernel(plan_ref, cache_ref, home_ref, asked_ref, cot_ref, new_ref, rows_ref, cots_ref,
-                 blocks, send_sem, recv_sem):
+def serve_kernel(n_hst, plan_ref, cache_ref, home_hbm, ask_ref, cot_ref, new_ref, rows_ref, cots_ref,
+                 blocks, home_ref, asked_ref, home_sem, send_sem, recv_sem):
+    home_copy = pltpu.make_async_copy(home_hbm, home_ref, home_sem)
+    home_copy.start()
     h, d = lax.axis_index("hst"), lax.axis_index("dev")
     y, x, c = d // 4, (d // 2) % 2, d % 2
     place = lambda a, b, e: a * 4 + b * 2 + e
     to_core, to_x, to_y = place(y, x, 1 - c), place(y, 1 - x, c), place(1 - y, x, c)
     to_diag = place(1 - y, 1 - x, c)
     peers = [(d + j) % 8 for j in range(1, 8)]
+    me = h * 8 + d
+    everyone = [(me + j) % (n_hst * 8) for j in range(1, n_hst * 8)]
 
     barrier = pltpu.get_barrier_semaphore()
-    for peer in peers:
-        pl.semaphore_signal(barrier, inc=1, device_id=(h, peer), device_id_type=pl.DeviceIdType.MESH)
-    pl.semaphore_wait(barrier, len(peers))
+    for q in everyone:
+        pl.semaphore_signal(
+            barrier, inc=1, device_id=(q // 8, q % 8), device_id_type=pl.DeviceIdType.MESH
+        )
+    pl.semaphore_wait(barrier, len(everyone))
 
     used = [0]
 
-    def send(src, dst, peer):
+    def send(src, dst, peer, plane=h):
         k = used[0]
         used[0] = k + 1
         copy = pltpu.make_async_remote_copy(
             src_ref=src, dst_ref=dst, send_sem=send_sem.at[k], recv_sem=recv_sem.at[k],
-            device_id=(h, peer), device_id_type=pl.DeviceIdType.MESH,
+            device_id=(plane, peer), device_id_type=pl.DeviceIdType.MESH,
         )
         copy.start()
         return copy
@@ -235,25 +241,40 @@
     own = lambda j, peer: send(cache_ref.at[j], blocks.at[d * CSLOT + j], peer)
     x_first, y_last = own(0, to_x), own(1, to_y)
     x_last, y_first = own(1, to_x), own(0, to_y)
+    asks = [send(ask_ref.at[q], asked_ref.at[me], q % 8, q // 8) for q in everyone]
     core = [own(0, to_core), own(1, to_core)]
     cots = [send(cot_ref.at[peer], cots_ref.at[d], peer) for peer in peers]
     for j in range(CSLOT):
         blocks[d * CSLOT + j] = cache_ref[j]
     cots_ref[d] = cot_ref[d]
+    asked_ref[me] = ask_ref[me]
 
     home_rows = home_ref.shape[0]
-    asked_rows = asked_ref.shape[0]
-    tile = 256
-    tiles = asked_rows // tile
+    slots = ask_ref.shape[2]
+    together = 4
+    tile = together * slots
+    tiles = asked_ref.shape[0] // together
     bf16 = rows_ref.dtype
-
-    def one_hot(rows, first, count):
+    diagonal = lax.broadcasted_iota(jnp.int32, (slots, slots), 0) == lax.broadcasted_iota(
+        jnp.int32, (slots, slots), 1
+    )
+
+    def column(p):
+        row = jnp.broadcast_to(asked_ref[p].astype(jnp.float32), (slots, slots))
+        return jnp.sum(jnp.where(diagonal, row, 0.0), axis=1, keepdims=True)
+
+    def one_hot(t, first, count):
+        asked = jnp.concatenate([column(t * together + u) for u in range(together)], 0)
         at = lax.broadcasted_iota(jnp.int32, (tile, count), 1) + first
-        return jnp.where(asked_ref[rows, :] == at, 1.0, 0.0).astype(bf16)
+        return jnp.where(asked == at.astype(jnp.float32), 1.0, 0.0).astype(bf16)
+
+    home_copy.wait()
+    for copy in asks:
+        copy.wait()
 
     def from_home(t):
         rows = pl.ds(pl.multiple_of(t * tile, tile), tile)
-        picked = jnp.dot(one_hot(rows, 0, home_rows), home_ref[...], preferred_element_type=jnp.float32)
+        picked = jnp.dot(one_hot(t, 0, home_rows), home_ref[...], preferred_element_type=jnp.float32)
         rows_ref[rows, :] = picked.astype(bf16)
 
     pl.loop(0, tiles // 2)(from_home)
@@ -284,28 +305,31 @@
     @pl.loop(0, tiles)
     def _(t):
         rows = pl.ds(pl.multiple_of(t * tile, tile), tile)
-        hot = one_hot(rows, home_rows, CSLOT * block)
+        hot = one_hot(t, home_rows, CSLOT * block)
         picked = jnp.dot(hot, new_ref[...], preferred_element_type=jnp.float32)
         rows_ref[rows, :] = (rows_ref[rows, :].astype(jnp.float32) + picked).astype(bf16)
 
 
-def serve_rows(plan, cache, home, asked, cot_parts):
+def serve_rows(n_hst, plan, cache, home, ask, cot_parts):
     _, block, width = cache.shape
     bf16 = jnp.bfloat16
-    asks = asked.shape[0]
+    asks = ask.shape[0] * ask.shape[2]
     vmem = pl.BlockSpec(memory_space=pltpu.VMEM)
-    copies = 21
+    copies = 20 + ask.shape[0]
     return pl.pallas_call(
-        serve_kernel,
+        functools.partial(serve_kernel, n_hst),
         out_shape=(
             jax.ShapeDtypeStruct((CSLOT * block, width), bf16),
             jax.ShapeDtypeStruct((asks, width), bf16),
             jax.ShapeDtypeStruct(cot_parts.shape, bf16),
         ),
-        in_specs=[pl.BlockSpec(memory_space=pltpu.SMEM)] + [vmem] * 4,
+        in_specs=[pl.BlockSpec(memory_space=pltpu.SMEM), vmem, pl.BlockSpec(memory_space=pl.ANY), vmem, vmem],
         out_specs=[vmem] * 3,
         scratch_shapes=[
             pltpu.VMEM((8 * CSLOT, block, width), bf16),
+            pltpu.VMEM(home.shape, bf16),
+            pltpu.VMEM(ask.shape, jnp.int32),
+            pltpu.SemaphoreType.DMA,
             pltpu.SemaphoreType.DMA((copies,)),
             pltpu.SemaphoreType.DMA((copies,)),
         ],
@@ -318,7 +342,7 @@
             transcendentals=0,
         ),
         name="serve_rows",
-    )(plan, cache, home, asked, cot_parts)
+    )(plan, cache, home, ask, cot_parts)
 
 
 def local(
@@ -350,14 +374,16 @@
     cache_rows = cache_blocks.shape[1]
     block = cache_rows // CSLOT
 
-    requests = lax.all_to_all(
-        miss_ids.reshape(device_count, slot_count), BOTH, split_axis=0, concat_axis=0, tiled=True
-    ).reshape(-1)
     cot_parts = cotangent.reshape(seeds, n_hst, n_dev, part).transpose(2, 0, 1, 3)
     cot_parts = cot_parts.reshape(n_dev, seeds, n_hst * part)
     if n_dev == 8:
         new_cache, row_data, cot_cols = serve_rows(
-            plan, cache_blocks.reshape(CSLOT, block, width_in), features, requests[:, None], cot_parts
+            n_hst,
+            plan,
+            cache_blocks.reshape(CSLOT, block, width_in),
+            features,
+            miss_ids.reshape(device_count, 1, slot_count),
+            cot_parts,
         )
         cot_cols = cot_cols.reshape(n_dev * seeds, n_hst * part)
     else:
@@ -365,6 +391,9 @@
         cot_cols = lax.all_to_all(
             cot_parts, "dev", split_axis=0, concat_axis=0, tiled=True
         ).reshape(n_dev * seeds, n_hst * part)
+        requests = lax.all_to_all(
+            miss_ids.reshape(device_count, slot_count), BOTH, split_axis=0, concat_axis=0, tiled=True
+        ).reshape(-1)
         from_home = features[jnp.minimum(requests, home_rows - 1)]
         blocks = everyones.reshape(-1, block, width_in)
         new_cache = jnp.concatenate(

time: 180 us -> 178 us (0.989)
  Pallas kernels: 55.9 us -> 69.9 us
  starting transfers between devices: 11.2 us -> 3.86 us
  waiting for transfers between devices: 46.7 us -> 41.7 us
  local copies, waits for them, and re-layouts: 20 us -> 17.3 us
    pallas_call x1, Pallas kernels: 21.2 us -> 35.3 us  [serve_rows(): pl.pallas_call(functools.partial(serve_kernel, n_hst), out_shape=(jax.Sha...]
    all_to_all x1 -> x0, starting transfers between devices: 7.3 us -> none  [local(): lax.all_to_all(miss_ids.reshape(device_count, slot_count), BOTH, split_ax...]
    all_to_all x1 -> x0, waiting for transfers between devices: 5.08 us -> none  [local(): lax.all_to_all(miss_ids.reshape(device_count, slot_count), BOTH, split_ax...]
    unnamed x43 -> x39, local copies, waits for them, and re-layouts: 9.17 us -> 8.42 us
  transfers between devices with their start and end apart: 2 -> 1, of which waited for: 2 -> 1; matrix products, arithmetic and copies ran while one was open for 18% -> 17% of each run, Pallas kernels for 0% -> 0%
where the time goes in v4:
time: 178 us
  Pallas kernels  69.9 us (39%)
  waiting for transfers between devices  41.7 us (23%)
  matrix products  22.5 us (13%)
  other arithmetic  21.5 us (12%)
  local copies, waits for them, and re-layouts  17.3 us (10%)
  starting transfers between devices  3.86 us (2%)
    all_to_all x1, waiting for transfers between devices, local(): lax.all_to_all(row_data.reshape(device_count, slot_count, width_in), BOTH...  41.7 us
    pallas_call x1, Pallas kernels, serve_rows(): pl.pallas_call(functools.partial(serve_kernel, n_hst), out_shape=(jax.Sha...  35.3 us
    pallas_call x1, Pallas kernels, sum_over_devices(): pl.pallas_call(functools.partial(sum_kernel, n_hst), out_shape=(jax.Shape...  34.6 us
    convert_element_type x1, other arithmetic, pick_matrix(): return jnp.where(valid[:, None], total, 0.0).astype(dtype)  17.3 us
    dot_general x6, matrix products, contract(): lax.dot_general(left, right, (((dim_left,), (dim_right,)), ((), ())), pre...  15.8 us
    unnamed x39, local copies, waits for them, and re-layouts  8.42 us
    mul x2, local copies, waits for them, and re-layouts, local(): back_mean[:, None, :] * used_two[:, :, None]  6.11 us
    mul x1, other arithmetic, local(): back_mean[:, None, :] * used_two[:, :, None]  4.01 us
  transfers between devices with their start and end apart: 1, of which 1 were waited for; matrix products, arithmetic and copies ran while one was open for 17% of the time, Pallas kernels for 0%

profile of v4, /device:TPU:0, one launch (start us, length us, event | category | flops | bytes accessed | tf_op | source)
XLA Modules:
  0.0 177.6 jit_solution(13950777664486480516)
XLA Ops:
  0.6 1.2 reshape.86
  2.0 0.2 reshape.87.cot_ref
  2.2 1.9 %copy-done.2 = bf16[2048,768]{1,0:T(8,128)(2,1)S(1)} copy-done((bf16[2048,768]{1,0:T(8,128)(2,1)S(1)}, bf16[2048,768]{1,0:T(8,128)(2,1)}, u32[]{:S(2)}) %copy-start.2) | copy-done | bytes 3145752
  4.1 1.0 copy-done.3
  5.0 0.7 copy-done.4
  5.8 0.7 copy-done.5
  6.4 35.3 %serve_rows.1 = (bf16[256,768]{1,0:T(8,128)(2,1)S(1)}, bf16[2048,768]{1,0:T(8,128)(2,1)S(1)}, bf16[8,32,128]{2,1,0:T(8,128)(2,1)S(1)}) custom-call(s32[1,2]{1,0:T(1,128)S(1)} %copy-done.5, bf16[2,128,768]{2,1,0:T(8,128)(2,1)S(1)} %bitcast.48, bf16[2048,768]{1,0:T(8,128)(2,1)S(1)} %copy-done.2, s32[32,1,64]{2,1,0:T(1,128)S(1)} %bitcast.49, ...), custom_call_target="tpu_custom_call" | custom-call | flops 7247757312 | bytes 12582912 | tf_op jit(solution)/shard_map/serve_rows/pallas_call | solution.py:319
  41.7 1.6 copy-done.1
  43.4 3.9 %all-to-all-start = ((bf16[32,64,768]{2,1,0:T(8,128)(2,1)}), bf16[32,64,768]{2,1,0:T(8,128)(2,1)}, u32[]{:S(2)}, u32[]{:S(2)}) async-start(bf16[32,64,768]{2,1,0:T(8,128)(2,1)} %bitcast.40), calls=%async_computation | async-start | bytes 6291456 | tf_op jit(solution)/shard_map/all_to_all | solution.py:406
  47.5 0.1 slice_reduce_fusion.14
  47.7 17.3 %select_convert_fusion = (bf16[832,2048]{1,0:T(8,128)(2,1)}, bf16[832,2048]{1,0:T(8,128)(2,1)}) fusion(s32[832]{0:T(1024)S(1)} %copy-done.13, pred[2048]{0:T(1024)(128)(4,1)S(1)} %lt.49, s32[832]{0:T(1024)S(1)} %get-tuple-element.23, s32[832]{0:T(1024)S(1)} %get-tuple-element.24, s32[832]{0:T(1024)S(1)} %get-tuple-element.25, s32[832]{0:T(1024)S(1)} %get-tuple-element.26, ...), kind=kLoop, calls=%fused_computation | loop fusion | flops 85196800 | bytes 6871040 | tf_op jit(solution)/shard_map/convert_element_type | solution.py:21
  65.0 0.7 convolution_divide_fusion
  65.8 2.5 %mul.40 = f32[32,25,1024]{2,1,0:T(8,128)} broadcast(f32[32,1024]{1,0:T(8,128)S(1)} %convolution_divide_fusion), dimensions={0,2} | broadcast | bytes 3407872 | tf_op jit(solution)/shard_map/mul | solution.py:424
  68.2 3.6 %mul.41 = f32[800,1024]{1,0:T(8,128)} reshape(f32[32,25,1024]{2,1,0:T(8,128)} %mul.40) | data formatting | bytes 6553600 | tf_op jit(solution)/shard_map/mul | solution.py:424
  72.2 0.7 fusion.15
  72.9 4.0 %broadcast_multiply_fusion = f32[800,1024]{1,0:T(8,128)} fusion(f32[800,1024]{1,0:T(8,128)} %mul.41, f32[800]{0:T(1024)S(1)} %reshape.93), kind=kLoop, calls=%fused_computation.27 | loop fusion | flops 819200 | bytes 6556800 | tf_op jit(solution)/shard_map/mul | solution.py:424
  76.9 41.7 %all-to-all-done = bf16[32,64,768]{2,1,0:T(8,128)(2,1)} async-done(((bf16[32,64,768]{2,1,0:T(8,128)(2,1)}), bf16[32,64,768]{2,1,0:T(8,128)(2,1)}, u32[]{:S(2)}, u32[]{:S(2)}) %all-to-all-start) | async-done | bytes 3145760 | tf_op jit(solution)/shard_map/all_to_all | solution.py:406
  118.6 5.8 %convolution_convert_fusion.2 = bf16[832,768]{1,0:T(8,128)(2,1)S(1)} fusion(bf16[832,2048]{1,0:T(8,128)(2,1)} %get-tuple-element.14, bf16[2048,768]{1,0:T(8,128)(2,1)} %bitcast.5), kind=kOutput, calls=%fused_computation.28 | convolution fusion | flops 2617884672 | bytes 7831552 | tf_op jit(solution)/shard_map/dot_general | solution.py:25
  124.4 1.5 fusion.14
  125.9 0.5 copy-done.8
  126.4 4.9 %divide_convert_fusion = bf16[832,768]{1,0:T(8,128)(2,1)S(1)} fusion(bf16[832,2048]{1,0:T(8,128)(2,1)S(1)} %copy-done.8, bf16[2048,768]{1,0:T(8,128)(2,1)} %bitcast.5, f32[832]{0:T(1024)S(1)} %convert_element_type.52), kind=kOutput, calls=%fused_computation.23 | convolution fusion | flops 2618523648 | bytes 7834880 | tf_op jit(solution)/shard_map/dot_general | solution.py:25
  131.3 3.1 %fusion.1 = (bf16[832,1024]{1,0:T(8,128)(2,1)S(1)}, bf16[832,1024]{1,0:T(8,128)(2,1)S(1)}) fusion(f32[800,1024]{1,0:T(8,128)S(1)} %copy-done.9, f32[32,1024]{1,0:T(8,128)S(1)} %fusion.15, f32[832,1024]{1,0:T(8,128)S(1)} %fusion.14, bf16[832,768]{1,0:T(8,128)(2,1)S(1)} %divide_convert_fusion, bf16[768,1024]{1,0:T(8,128)(2,1)S(1)} %copy-done.17), kind=kOutput, calls=%fused_computation.20 | convolution fusion | flops 1319698432 | bytes 13074432 | tf_op jit(solution)/shard_map/dot_general | solution.py:429
  134.4 1.9 %convolution_convert_fusion = bf16[1024,768]{1,0:T(8,128)(2,1)S(1)} fusion(bf16[832,1024]{1,0:T(8,128)(2,1)S(1)} %get-tuple-element.37, bf16[832,768]{1,0:T(8,128)(2,1)S(1)} %divide_convert_fusion), kind=kOutput, calls=%fused_computation.25 | convolution fusion | flops 1309409280 | bytes 4554752 | tf_op jit(solution)/shard_map/dot_general | solution.py:25
  136.3 1.9 %convolution_convert_fusion.1 = bf16[1024,768]{1,0:T(8,128)(2,1)S(1)} fusion(bf16[832,1024]{1,0:T(8,128)(2,1)S(1)} %get-tuple-element.37, bf16[832,768]{1,0:T(8,128)(2,1)S(1)} %convolution_convert_fusion.2), kind=kOutput, calls=%fused_computation.26 | convolution fusion | flops 1309409280 | bytes 4554752 | tf_op jit(solution)/shard_map/dot_general | solution.py:25
  138.2 0.5 fusion.12
  138.6 0.4 fusion.2
  139.1 34.6 %sum_over_devices.1 = (f32[32,768]{1,0:T(8,128)S(1)}, f32[32,768]{1,0:T(8,128)S(1)}, f32[32,2048]{1,0:T(8,128)S(1)}) custom-call(bf16[16,2,32,768]{3,2,1,0:T(8,128)(2,1)S(1)} %bitcast.42, bf16[16,2,32,768]{3,2,1,0:T(8,128)(2,1)S(1)} %bitcast.41, bf16[32,2048]{1,0:T(8,128)(2,1)S(1)} %pad_maximum_fusion.rows_ref, bf16[128,256]{1,0:T(8,128)(2,1)S(1)} %bitcast.44), custom_call_target="tpu_custom_call" | custom-call | flops 134217728 | bytes 6291456 | tf_op jit(solution)/shard_map/sum_over_devices/pallas_call | solution.py:162
  173.8 0.7 slice_bitcast_fusion
  174.5 1.1 fusion.3
  175.6 0.7 copy.29
  176.3 0.6 copy.30
  177.0 0.6 copy.31
  (43 shorter events, 0.7 us)
Async XLA Ops:
  0.6 71.5 %copy-start = (bf16[1024,1024]{1,0:T(8,128)(2,1)S(1)}, bf16[1024,1024]{1,0:T(8,128)(2,1)}, u32[]{:S(2)}) copy-start(bf16[1024,1024]{1,0:T(8,128)(2,1)} %param.25) | copy-start | bytes 6291460
  2.2 1.9 %copy-start.2 = (bf16[2048,768]{1,0:T(8,128)(2,1)S(1)}, bf16[2048,768]{1,0:T(8,128)(2,1)}, u32[]{:S(2)}) copy-start(bf16[2048,768]{1,0:T(8,128)(2,1)} %home_hbm.1) | copy-start | bytes 9437188
  4.1 1.0 copy-start.3
  5.0 0.7 copy-start.4
  5.8 0.7 copy-start.5
  41.7 1.6 copy-start.1
  43.3 3.9 %copy-start.14 = (s32[1,4,8]{2,1,0:T(4,128)S(1)}, s32[1,4,8]{2,1,0:T(4,128)}, u32[]{:S(2)}) copy-start(s32[1,4,8]{2,1,0:T(4,128)} %param.18) | copy-start | bytes 388
  43.3 4.1 %copy-start.12 = (s32[832]{0:T(1024)S(1)}, s32[832]{0:T(1024)}, u32[]{:S(2)}) copy-start(s32[832]{0:T(1024)} %param.21) | copy-start | bytes 9988
  43.4 4.1 %copy-start.11 = (s32[832,15]{0,1:T(8,128)S(1)}, s32[832,15]{0,1:T(8,128)}, u32[]{:S(2)}) copy-start(s32[832,15]{0,1:T(8,128)} %param.20) | copy-start | bytes 149764
  43.4 4.3 %copy-start.13 = (s32[832]{0:T(1024)S(1)}, s32[832]{0:T(1024)}, u32[]{:S(2)}) copy-start(s32[832]{0:T(1024)} %param.19) | copy-start | bytes 9988
  43.4 75.2 %all-to-all-start = ((bf16[32,64,768]{2,1,0:T(8,128)(2,1)}), bf16[32,64,768]{2,1,0:T(8,128)(2,1)}, u32[]{:S(2)}, u32[]{:S(2)}) async-start(bf16[32,64,768]{2,1,0:T(8,128)(2,1)} %bitcast.40), calls=%async_computation | async-start | bytes 6291456 | tf_op jit(solution)/shard_map/all_to_all | solution.py:406
  47.7 17.3 %copy-start.15 = (s32[32]{0:T(128)S(1)}, s32[32]{0:T(128)}, u32[]{:S(2)}) copy-start(s32[32]{0:T(128)} %param.22) | copy-start | bytes 388
  47.7 17.3 %copy-start.6 = (bf16[1024,1024]{1,0:T(8,128)(2,1)S(1)}, bf16[1024,1024]{1,0:T(8,128)(2,1)}, u32[]{:S(2)}) copy-start(bf16[1024,1024]{1,0:T(8,128)(2,1)} %param.26) | copy-start | bytes 6291460
  47.7 17.3 %copy-start.10 = (bf16[32,1024]{1,0:T(8,128)(2,1)S(1)}, bf16[32,1024]{1,0:T(8,128)(2,1)}, u32[]{:S(2)}) copy-start(bf16[32,1024]{1,0:T(8,128)(2,1)} %param.27) | copy-start | bytes 196612
  118.6 5.8 %copy-start.16 = (bf16[768,1024]{1,0:T(8,128)(2,1)S(1)}, bf16[768,1024]{1,0:T(8,128)(2,1)}, u32[]{:S(2)}) copy-start(bf16[768,1024]{1,0:T(8,128)(2,1)} %param.23) | copy-start | bytes 4718596
  124.4 2.0 %copy-start.8 = (bf16[832,2048]{1,0:T(8,128)(2,1)S(1)}, bf16[832,2048]{1,0:T(8,128)(2,1)}, u32[]{:S(2)}) copy-start(bf16[832,2048]{1,0:T(8,128)(2,1)} %get-tuple-element.16) | copy-start | bytes 10223620
  126.4 4.9 %copy-start.9 = (f32[800,1024]{1,0:T(8,128)S(1)}, f32[800,1024]{1,0:T(8,128)}, u32[]{:S(2)}) copy-start(f32[800,1024]{1,0:T(8,128)} %broadcast_multiply_fusion) | copy-start | bytes 9830404
  126.4 4.9 %copy-start.17 = (bf16[768,1024]{1,0:T(8,128)(2,1)S(1)}, bf16[768,1024]{1,0:T(8,128)(2,1)}, u32[]{:S(2)}) copy-start(bf16[768,1024]{1,0:T(8,128)(2,1)} %param.24) | copy-start | bytes 4718596
  138.6 35.8 %copy-start.7 = (bf16[1024,1024]{1,0:T(8,128)(2,1)S(1)}, bf16[1024,1024]{1,0:T(8,128)(2,1)}, u32[]{:S(2)}) copy-start(bf16[1024,1024]{1,0:T(8,128)(2,1)} %param.26) | copy-start | bytes 6291460

commit v5 on v4

--- a/solution.py
+++ b/solution.py
@@ -239,9 +239,9 @@
         return send(slot, slot, peer)
 
     own = lambda j, peer: send(cache_ref.at[j], blocks.at[d * CSLOT + j], peer)
+    asks = [send(ask_ref.at[q], asked_ref.at[me], q % 8, q // 8) for q in everyone]
     x_first, y_last = own(0, to_x), own(1, to_y)
     x_last, y_first = own(1, to_x), own(0, to_y)
-    asks = [send(ask_ref.at[q], asked_ref.at[me], q % 8, q // 8) for q in everyone]
     core = [own(0, to_core), own(1, to_core)]
     cots = [send(cot_ref.at[peer], cots_ref.at[d], peer) for peer in peers]
     for j in range(CSLOT):
@@ -277,19 +277,23 @@
         picked = jnp.dot(one_hot(t, 0, home_rows), home_ref[...], preferred_element_type=jnp.float32)
         rows_ref[rows, :] = picked.astype(bf16)
 
-    pl.loop(0, tiles // 2)(from_home)
+    early, half = tiles // 4, tiles // 2
+    pl.loop(0, early)(from_home)
 
     x_first.wait()
     diag_first = pass_on(to_x, 0, to_y)
     y_last.wait()
     diag_last = pass_on(to_y, 1, to_x)
     core += [pass_on(to_x, 0, to_core), pass_on(to_y, 1, to_core)]
+
+    pl.loop(early, half)(from_home)
+
     x_last.wait()
     core.append(pass_on(to_x, 1, to_core))
     y_first.wait()
     core.append(pass_on(to_y, 0, to_core))
 
-    pl.loop(tiles // 2, tiles)(from_home)
+    pl.loop(half, tiles)(from_home)
 
     diag_first.wait()
     core.append(pass_on(to_diag, 0, to_core))

time: 178 us -> 172 us (0.966)
  Pallas kernels: 69.9 us -> 63.7 us
    pallas_call x1, Pallas kernels: 35.3 us -> 29.1 us  [serve_rows(): pl.pallas_call(functools.partial(serve_kernel, n_hst), out_shape=(jax.Sha...]
where the time goes in v5:
time: 172 us; the launch traced here: 171 us
  Pallas kernels  63.7 us (37%)
  waiting for transfers between devices  41.7 us (24%)
  matrix products  22.5 us (13%)
  other arithmetic  21.5 us (12%)
  local copies, waits for them, and re-layouts  17.3 us (10%)
  starting transfers between devices  3.86 us (2%)
    all_to_all x1, waiting for transfers between devices, local(): lax.all_to_all(row_data.reshape(device_count, slot_count, width_in), BOTH...  41.7 us
    pallas_call x1, Pallas kernels, sum_over_devices(): pl.pallas_call(functools.partial(sum_kernel, n_hst), out_shape=(jax.Shape...  34.6 us
    pallas_call x1, Pallas kernels, serve_rows(): pl.pallas_call(functools.partial(serve_kernel, n_hst), out_shape=(jax.Sha...  29.1 us
    convert_element_type x1, other arithmetic, pick_matrix(): return jnp.where(valid[:, None], total, 0.0).astype(dtype)  17.3 us
    dot_general x6, matrix products, contract(): lax.dot_general(left, right, (((dim_left,), (dim_right,)), ((), ())), pre...  15.8 us
    unnamed x39, local copies, waits for them, and re-layouts  8.42 us
    mul x2, local copies, waits for them, and re-layouts, local(): back_mean[:, None, :] * used_two[:, :, None]  6.11 us
    mul x1, other arithmetic, local(): back_mean[:, None, :] * used_two[:, :, None]  4.01 us
  transfers between devices with their start and end apart: 1, of which 1 were waited for; matrix products, arithmetic and copies ran while one was open for 17% of the time, Pallas kernels for 0%

profile of v5, /device:TPU:0, one launch (start us, length us, event | category | flops | bytes accessed | tf_op | source)
XLA Modules:
  0.0 171.4 jit_solution(6485702378537598867)
XLA Ops:
  0.6 1.2 reshape.86
  2.0 0.2 reshape.87.cot_ref
  2.2 1.9 %copy-done.2 = bf16[2048,768]{1,0:T(8,128)(2,1)S(1)} copy-done((bf16[2048,768]{1,0:T(8,128)(2,1)S(1)}, bf16[2048,768]{1,0:T(8,128)(2,1)}, u32[]{:S(2)}) %copy-start.2) | copy-done | bytes 3145752
  4.1 1.0 copy-done.3
  5.0 0.7 copy-done.4
  5.8 0.7 copy-done.5
  6.4 29.1 %serve_rows.1 = (bf16[256,768]{1,0:T(8,128)(2,1)S(1)}, bf16[2048,768]{1,0:T(8,128)(2,1)S(1)}, bf16[8,32,128]{2,1,0:T(8,128)(2,1)S(1)}) custom-call(s32[1,2]{1,0:T(1,128)S(1)} %copy-done.5, bf16[2,128,768]{2,1,0:T(8,128)(2,1)S(1)} %bitcast.48, bf16[2048,768]{1,0:T(8,128)(2,1)S(1)} %copy-done.2, s32[32,1,64]{2,1,0:T(1,128)S(1)} %bitcast.49, ...), custom_call_target="tpu_custom_call" | custom-call | flops 7247757312 | bytes 12582912 | tf_op jit(solution)/shard_map/serve_rows/pallas_call | solution.py:323
  35.5 1.6 copy-done.1
  37.1 3.9 %all-to-all-start = ((bf16[32,64,768]{2,1,0:T(8,128)(2,1)}), bf16[32,64,768]{2,1,0:T(8,128)(2,1)}, u32[]{:S(2)}, u32[]{:S(2)}) async-start(bf16[32,64,768]{2,1,0:T(8,128)(2,1)} %bitcast.40), calls=%async_computation | async-start | bytes 6291456 | tf_op jit(solution)/shard_map/all_to_all | solution.py:410
  41.3 0.1 slice_reduce_fusion.14
  41.5 17.3 %select_convert_fusion = (bf16[832,2048]{1,0:T(8,128)(2,1)}, bf16[832,2048]{1,0:T(8,128)(2,1)}) fusion(s32[832]{0:T(1024)S(1)} %copy-done.13, pred[2048]{0:T(1024)(128)(4,1)S(1)} %lt.49, s32[832]{0:T(1024)S(1)} %get-tuple-element.23, s32[832]{0:T(1024)S(1)} %get-tuple-element.24, s32[832]{0:T(1024)S(1)} %get-tuple-element.25, s32[832]{0:T(1024)S(1)} %get-tuple-element.26, ...), kind=kLoop, calls=%fused_computation | loop fusion | flops 85196800 | bytes 6871040 | tf_op jit(solution)/shard_map/convert_element_type | solution.py:21
  58.8 0.7 convolution_divide_fusion
  59.5 2.5 %mul.40 = f32[32,25,1024]{2,1,0:T(8,128)} broadcast(f32[32,1024]{1,0:T(8,128)S(1)} %convolution_divide_fusion), dimensions={0,2} | broadcast | bytes 3407872 | tf_op jit(solution)/shard_map/mul | solution.py:428
  62.0 3.6 %mul.41 = f32[800,1024]{1,0:T(8,128)} reshape(f32[32,25,1024]{2,1,0:T(8,128)} %mul.40) | data formatting | bytes 6553600 | tf_op jit(solution)/shard_map/mul | solution.py:428
  66.0 0.7 fusion.15
  66.7 4.0 %broadcast_multiply_fusion = f32[800,1024]{1,0:T(8,128)} fusion(f32[800,1024]{1,0:T(8,128)} %mul.41, f32[800]{0:T(1024)S(1)} %reshape.93), kind=kLoop, calls=%fused_computation.27 | loop fusion | flops 819200 | bytes 6556800 | tf_op jit(solution)/shard_map/mul | solution.py:428
  70.7 41.7 %all-to-all-done = bf16[32,64,768]{2,1,0:T(8,128)(2,1)} async-done(((bf16[32,64,768]{2,1,0:T(8,128)(2,1)}), bf16[32,64,768]{2,1,0:T(8,128)(2,1)}, u32[]{:S(2)}, u32[]{:S(2)}) %all-to-all-start) | async-done | bytes 3145760 | tf_op jit(solution)/shard_map/all_to_all | solution.py:410
  112.4 5.8 %convolution_convert_fusion.2 = bf16[832,768]{1,0:T(8,128)(2,1)S(1)} fusion(bf16[832,2048]{1,0:T(8,128)(2,1)} %get-tuple-element.14, bf16[2048,768]{1,0:T(8,128)(2,1)} %bitcast.5), kind=kOutput, calls=%fused_computation.28 | convolution fusion | flops 2617884672 | bytes 7831552 | tf_op jit(solution)/shard_map/dot_general | solution.py:25
  118.2 1.5 fusion.14
  119.7 0.5 copy-done.8
  120.2 4.9 %divide_convert_fusion = bf16[832,768]{1,0:T(8,128)(2,1)S(1)} fusion(bf16[832,2048]{1,0:T(8,128)(2,1)S(1)} %copy-done.8, bf16[2048,768]{1,0:T(8,128)(2,1)} %bitcast.5, f32[832]{0:T(1024)S(1)} %convert_element_type.52), kind=kOutput, calls=%fused_computation.23 | convolution fusion | flops 2618523648 | bytes 7834880 | tf_op jit(solution)/shard_map/dot_general | solution.py:25
  125.1 3.1 %fusion.1 = (bf16[832,1024]{1,0:T(8,128)(2,1)S(1)}, bf16[832,1024]{1,0:T(8,128)(2,1)S(1)}) fusion(f32[800,1024]{1,0:T(8,128)S(1)} %copy-done.9, f32[32,1024]{1,0:T(8,128)S(1)} %fusion.15, f32[832,1024]{1,0:T(8,128)S(1)} %fusion.14, bf16[832,768]{1,0:T(8,128)(2,1)S(1)} %divide_convert_fusion, bf16[768,1024]{1,0:T(8,128)(2,1)S(1)} %copy-done.17), kind=kOutput, calls=%fused_computation.20 | convolution fusion | flops 1319698432 | bytes 13074432 | tf_op jit(solution)/shard_map/dot_general | solution.py:433
  128.2 1.9 %convolution_convert_fusion = bf16[1024,768]{1,0:T(8,128)(2,1)S(1)} fusion(bf16[832,1024]{1,0:T(8,128)(2,1)S(1)} %get-tuple-element.37, bf16[832,768]{1,0:T(8,128)(2,1)S(1)} %divide_convert_fusion), kind=kOutput, calls=%fused_computation.25 | convolution fusion | flops 1309409280 | bytes 4554752 | tf_op jit(solution)/shard_map/dot_general | solution.py:25
  130.1 1.9 %convolution_convert_fusion.1 = bf16[1024,768]{1,0:T(8,128)(2,1)S(1)} fusion(bf16[832,1024]{1,0:T(8,128)(2,1)S(1)} %get-tuple-element.37, bf16[832,768]{1,0:T(8,128)(2,1)S(1)} %convolution_convert_fusion.2), kind=kOutput, calls=%fused_computation.26 | convolution fusion | flops 1309409280 | bytes 4554752 | tf_op jit(solution)/shard_map/dot_general | solution.py:25
  131.9 0.5 fusion.12
  132.4 0.4 fusion.2
  132.9 34.6 %sum_over_devices.1 = (f32[32,768]{1,0:T(8,128)S(1)}, f32[32,768]{1,0:T(8,128)S(1)}, f32[32,2048]{1,0:T(8,128)S(1)}) custom-call(bf16[16,2,32,768]{3,2,1,0:T(8,128)(2,1)S(1)} %bitcast.42, bf16[16,2,32,768]{3,2,1,0:T(8,128)(2,1)S(1)} %bitcast.41, bf16[32,2048]{1,0:T(8,128)(2,1)S(1)} %pad_maximum_fusion.rows_ref, bf16[128,256]{1,0:T(8,128)(2,1)S(1)} %bitcast.44), custom_call_target="tpu_custom_call" | custom-call | flops 134217728 | bytes 6291456 | tf_op jit(solution)/shard_map/sum_over_devices/pallas_call | solution.py:162
  167.5 0.7 slice_bitcast_fusion
  168.2 1.1 fusion.3
  169.3 0.7 copy.29
  170.1 0.6 copy.30
  170.7 0.6 copy.31
  (43 shorter events, 0.7 us)
Async XLA Ops:
  0.6 65.3 %copy-start = (bf16[1024,1024]{1,0:T(8,128)(2,1)S(1)}, bf16[1024,1024]{1,0:T(8,128)(2,1)}, u32[]{:S(2)}) copy-start(bf16[1024,1024]{1,0:T(8,128)(2,1)} %param.25) | copy-start | bytes 6291460
  2.2 1.9 %copy-start.2 = (bf16[2048,768]{1,0:T(8,128)(2,1)S(1)}, bf16[2048,768]{1,0:T(8,128)(2,1)}, u32[]{:S(2)}) copy-start(bf16[2048,768]{1,0:T(8,128)(2,1)} %home_hbm.1) | copy-start | bytes 9437188
  4.1 1.0 copy-start.3
  5.0 0.7 copy-start.4
  5.8 0.7 copy-start.5
  35.5 1.6 copy-start.1
  37.1 3.9 %copy-start.14 = (s32[1,4,8]{2,1,0:T(4,128)S(1)}, s32[1,4,8]{2,1,0:T(4,128)}, u32[]{:S(2)}) copy-start(s32[1,4,8]{2,1,0:T(4,128)} %param.18) | copy-start | bytes 388
  37.1 4.1 %copy-start.12 = (s32[832]{0:T(1024)S(1)}, s32[832]{0:T(1024)}, u32[]{:S(2)}) copy-start(s32[832]{0:T(1024)} %param.21) | copy-start | bytes 9988
  37.1 4.1 %copy-start.11 = (s32[832,15]{0,1:T(8,128)S(1)}, s32[832,15]{0,1:T(8,128)}, u32[]{:S(2)}) copy-start(s32[832,15]{0,1:T(8,128)} %param.20) | copy-start | bytes 149764
  37.1 4.3 %copy-start.13 = (s32[832]{0:T(1024)S(1)}, s32[832]{0:T(1024)}, u32[]{:S(2)}) copy-start(s32[832]{0:T(1024)} %param.19) | copy-start | bytes 9988
  37.1 75.2 %all-to-all-start = ((bf16[32,64,768]{2,1,0:T(8,128)(2,1)}), bf16[32,64,768]{2,1,0:T(8,128)(2,1)}, u32[]{:S(2)}, u32[]{:S(2)}) async-start(bf16[32,64,768]{2,1,0:T(8,128)(2,1)} %bitcast.40), calls=%async_computation | async-start | bytes 6291456 | tf_op jit(solution)/shard_map/all_to_all | solution.py:410
  41.5 17.3 %copy-start.15 = (s32[32]{0:T(128)S(1)}, s32[32]{0:T(128)}, u32[]{:S(2)}) copy-start(s32[32]{0:T(128)} %param.22) | copy-start | bytes 388
  41.5 17.3 %copy-start.6 = (bf16[1024,1024]{1,0:T(8,128)(2,1)S(1)}, bf16[1024,1024]{1,0:T(8,128)(2,1)}, u32[]{:S(2)}) copy-start(bf16[1024,1024]{1,0:T(8,128)(2,1)} %param.26) | copy-start | bytes 6291460
  41.5 17.3 %copy-start.10 = (bf16[32,1024]{1,0:T(8,128)(2,1)S(1)}, bf16[32,1024]{1,0:T(8,128)(2,1)}, u32[]{:S(2)}) copy-start(bf16[32,1024]{1,0:T(8,128)(2,1)} %param.27) | copy-start | bytes 196612
  112.4 5.8 %copy-start.16 = (bf16[768,1024]{1,0:T(8,128)(2,1)S(1)}, bf16[768,1024]{1,0:T(8,128)(2,1)}, u32[]{:S(2)}) copy-start(bf16[768,1024]{1,0:T(8,128)(2,1)} %param.23) | copy-start | bytes 4718596
  118.2 2.0 %copy-start.8 = (bf16[832,2048]{1,0:T(8,128)(2,1)S(1)}, bf16[832,2048]{1,0:T(8,128)(2,1)}, u32[]{:S(2)}) copy-start(bf16[832,2048]{1,0:T(8,128)(2,1)} %get-tuple-element.16) | copy-start | bytes 10223620
  120.2 4.9 %copy-start.9 = (f32[800,1024]{1,0:T(8,128)S(1)}, f32[800,1024]{1,0:T(8,128)}, u32[]{:S(2)}) copy-start(f32[800,1024]{1,0:T(8,128)} %broadcast_multiply_fusion) | copy-start | bytes 9830404
  120.2 4.9 %copy-start.17 = (bf16[768,1024]{1,0:T(8,128)(2,1)S(1)}, bf16[768,1024]{1,0:T(8,128)(2,1)}, u32[]{:S(2)}) copy-start(bf16[768,1024]{1,0:T(8,128)(2,1)} %param.24) | copy-start | bytes 4718596
  132.4 35.8 %copy-start.7 = (bf16[1024,1024]{1,0:T(8,128)(2,1)S(1)}, bf16[1024,1024]{1,0:T(8,128)(2,1)}, u32[]{:S(2)}) copy-start(bf16[1024,1024]{1,0:T(8,128)(2,1)} %param.26) | copy-start | bytes 6291460
